TPU v7x, 256 devices: a whole 4x4x8 slice. The times are simulated.
256 devices in a mesh: pb: 8 (over x, y_lo), pa: 32 (over y_hi, z, core).
Axes of the slice: x: 4, y: 4 (y_hi: 2, y_lo: 2; y = y_hi * 2 + y_lo), z: 8, core: 2. Of those that a mesh axis runs over, the one named last changes fastest.
Arguments:
- questions: bfloat16 [16384, 4096], P(('pb', 'pa')), may hold values from -1 to 1
- passages: bfloat16 [16384, 4096], P(('pa', 'pb')), may hold values from -1 to 1
- hard_rows: bfloat16 [16384, 4096], P(('pa', 'pb')), may hold values from -1 to 1
- hard_index: int32 [16384], P('pb'), may hold values from 0 to 16383, as said below
- projection: bfloat16 [4096, 768], replicated, may hold values from -0.09375 to 0.09375
Outputs:
- grad_questions: bfloat16 [16384, 4096], P(('pb', 'pa'))
- grad_passages: bfloat16 [16384, 4096], P(('pa', 'pb'))
- grad_hard: bfloat16 [16384, 4096], P(('pa', 'pb'))
- question_loss: float32 [16384], P(('pb', 'pa'))
- passage_loss: float32 [16384], P(('pa', 'pb'))
Inputs may be any that keep to these rules, and one draw needn't show every extreme that they name: `hard_index`: the rows come in aligned blocks of 512 questions; the hard negative of a question lies in the same aligned block of 512 rows of hard_rows, and within a block every hard row is named by exactly one question.
All inputs are finite; a program needn't handle non-finite values.
Results may differ from a plain program's by a relative error of at most 0.024.
Values may be sent and summed in bfloat16 or wider, within the bound.
A program may use at most 128 MiB of HBM per device.

v0:
```python
import jax
import jax.numpy as jnp
from jax import lax
from jax.sharding import PartitionSpec as P

inverse_temp = 40.0
epsilon = 1e-06


def project_rows(pooled, projection):
    embedded = jnp.dot(pooled, projection, preferred_element_type=jnp.float32)
    inv_norm = lax.rsqrt(jnp.sum(embedded * embedded, axis=1, keepdims=True) + epsilon)
    return (embedded * inv_norm, inv_norm)


def unit_grad(grad_unit, unit_rows, inv_norm):
    along_unit = jnp.sum(grad_unit * unit_rows, axis=1, keepdims=True)
    return ((grad_unit - unit_rows * along_unit) * inv_norm).astype(jnp.bfloat16)


def column_product(tile_low, question_block):
    return lax.dot_general(
        tile_low, question_block, (((0,), (0,)), ((), ())), preferred_element_type=jnp.float32
    )


def shards(questions, passages, hard_rows, hard_index, projection):
    local_rows = questions.shape[0]
    stacked = jnp.concatenate([questions, passages, hard_rows], axis=0)
    unit_rows, inv_norm = project_rows(stacked, projection)
    unit_low = unit_rows.astype(jnp.bfloat16)
    question_block = lax.all_gather(unit_low[:local_rows], "pa", axis=0, tiled=True)
    passage_block, hard_block = (
        lax.all_gather(unit_low[local_rows : 2 * local_rows], "pb", axis=0, tiled=True),
        lax.all_gather(unit_low[2 * local_rows :], "pb", axis=0, tiled=True),
    )
    width_row = lax.axis_size("pb")
    width_col = lax.axis_size("pa")
    rank_row = lax.axis_index("pb")
    rank_col = lax.axis_index("pa")
    question_count = question_block.shape[0]
    passage_count = passage_block.shape[0]
    embed_width = question_block.shape[1]
    row_start = rank_row * question_count
    column_start = rank_col * passage_count
    score_tile = inverse_temp * jnp.einsum(
        "qd,pd->qp", question_block, passage_block, preferred_element_type=jnp.float32
    )
    row_ids = row_start + lax.broadcasted_iota(jnp.int32, (question_count, passage_count), 0)
    column_ids = column_start + lax.broadcasted_iota(jnp.int32, (question_count, passage_count), 1)
    diagonal = row_ids == column_ids
    exp_tile = jnp.exp(score_tile - inverse_temp)
    diag_score = jnp.where(diagonal, score_tile, 0.0)
    block_ratio = question_count // passage_count
    owner_flag = (rank_col // block_ratio == rank_row).astype(jnp.float32)
    offset = rank_col % block_ratio * passage_count
    paired_rows = lax.dynamic_slice_in_dim(question_block, offset, passage_count, 0)
    local_index = jnp.clip(
        lax.dynamic_slice_in_dim(hard_index, offset, passage_count, 0) - column_start,
        0,
        passage_count - 1,
    )
    hard_chosen = jnp.take(hard_block, local_index, axis=0)
    hard_score = inverse_temp * jnp.sum(
        paired_rows.astype(jnp.float32) * hard_chosen.astype(jnp.float32), axis=1
    )
    hard_exp = jnp.exp(hard_score - inverse_temp) * owner_flag
    row_part = jnp.sum(exp_tile, axis=1) + lax.dynamic_update_slice(
        jnp.zeros((question_count,), jnp.float32), hard_exp, (offset,)
    )
    column_part = jnp.sum(exp_tile, axis=0)
    exp_low = exp_tile.astype(jnp.bfloat16)
    question_share = question_count // width_col
    passage_share = passage_count // width_row
    question_first = rank_col * question_share
    passage_first = rank_row * passage_share
    batch_rows = question_count * width_row
    zero_rows = jnp.zeros((batch_rows,), jnp.float32)
    row_all, column_all, diag_all = lax.psum(
        (
            lax.dynamic_update_slice(zero_rows, row_part, (row_start,)),
            lax.dynamic_update_slice(zero_rows, column_part, (column_start,)),
            lax.dynamic_update_slice(zero_rows, jnp.sum(diag_score, axis=1), (row_start,)),
        ),
        ("pb", "pa"),
    )
    row_total = lax.dynamic_slice_in_dim(row_all, row_start, question_count, 0)
    column_total = lax.dynamic_slice_in_dim(column_all, column_start, passage_count, 0)
    row_diag = lax.dynamic_slice_in_dim(diag_all, row_start, question_count, 0)
    column_diag = lax.dynamic_slice_in_dim(diag_all, column_start, passage_count, 0)
    question_loss = (
        inverse_temp
        + jnp.log(lax.dynamic_slice_in_dim(row_total, question_first, question_share, 0))
        - lax.dynamic_slice_in_dim(row_diag, question_first, question_share, 0)
    )
    passage_loss = (
        inverse_temp
        + jnp.log(lax.dynamic_slice_in_dim(column_total, passage_first, passage_share, 0))
        - lax.dynamic_slice_in_dim(column_diag, passage_first, passage_share, 0)
    )
    target_twice = jnp.where(diagonal, 2.0, 0.0)
    column_low = (exp_tile / column_total[None, :] - target_twice).astype(jnp.bfloat16)
    row_low = (exp_tile / row_total[:, None] - target_twice).astype(jnp.bfloat16)
    hard_weight = hard_exp / lax.dynamic_slice_in_dim(row_total, offset, passage_count, 0)
    hard_question = lax.dynamic_update_slice(
        jnp.zeros((question_count, embed_width), jnp.float32),
        hard_weight[:, None] * hard_chosen.astype(jnp.float32),
        (offset, 0),
    )
    hard_passage = (
        jnp.zeros((passage_count, embed_width), jnp.float32)
        .at[local_index]
        .add(hard_weight[:, None] * paired_rows.astype(jnp.float32))
    )
    plain_sum = jnp.dot(exp_low, passage_block, preferred_element_type=jnp.float32)
    mixed_sum = jnp.dot(column_low, passage_block, preferred_element_type=jnp.float32)
    grad_question = lax.psum_scatter(
        (inverse_temp * (plain_sum / row_total[:, None] + mixed_sum + hard_question)).astype(
            jnp.bfloat16
        ),
        "pa",
        scatter_dimension=0,
        tiled=True,
    ).astype(jnp.float32)
    plain_sum = column_product(exp_low, question_block)
    mixed_sum = column_product(row_low, question_block)
    passage_sums = lax.psum_scatter(
        jnp.concatenate(
            [
                inverse_temp * (plain_sum / column_total[:, None] + mixed_sum),
                inverse_temp * hard_passage,
            ],
            axis=1,
        ).astype(jnp.bfloat16),
        "pb",
        scatter_dimension=0,
        tiled=True,
    ).astype(jnp.float32)
    grad_passage = passage_sums[:, :embed_width]
    grad_hard_unit = passage_sums[:, embed_width:]
    grad_unit = jnp.concatenate([grad_question, grad_passage, grad_hard_unit], axis=0)
    grad_embed = unit_grad(grad_unit, unit_rows, inv_norm)
    gradients = lax.dot_general(
        grad_embed, projection, (((1,), (1,)), ((), ())), preferred_element_type=jnp.float32
    ).astype(jnp.bfloat16)
    return (
        gradients[:local_rows],
        gradients[local_rows : 2 * local_rows],
        gradients[2 * local_rows :],
        question_loss,
        passage_loss,
    )


def solution(mesh):
    in_specs = (P(("pb", "pa"), None), P(("pa", "pb"), None), P(("pa", "pb"), None), P("pb"), P())
    out_specs = (
        P(("pb", "pa"), None),
        P(("pa", "pb"), None),
        P(("pa", "pb"), None),
        P(("pb", "pa")),
        P(("pa", "pb")),
    )
    return jax.shard_map(shards, mesh=mesh, in_specs=in_specs, out_specs=out_specs, check_vma=False)
```

profile of v0, /device:TPU:6, one launch (start us, length us, event | category | flops | bytes accessed | tf_op | source)
XLA Modules:
  0.0 557.1 jit_solution(116342709025801021)
XLA Ops:
  7.2 4.8 multiply_reduce_fusion.1
  12.0 0.9 copy-done.1
  13.8 0.8 compare_and_fusion
  14.5 29.6 %all_gather.11 = bf16[512,768]{1,0:T(8,128)(2,1)S(1)} all-gather(bf16[64,768]{1,0:T(8,128)(2,1)S(1)} %get-tuple-element.16), channel_id=1, replica_groups=mesh['pb'=8,'pa'=32] {'pb'}, dimensions={0}, use_global_device_ids=true | all-gather | bytes 884736 | tf_op jit(solution)/shard_map/all_gather | solution.py:35
  44.2 2.0 gather_fusion
  46.2 30.5 %all_gather.10 = bf16[512,768]{1,0:T(8,128)(2,1)S(1)} all-gather(bf16[64,768]{1,0:T(8,128)(2,1)S(1)} %get-tuple-element.17), channel_id=1, replica_groups=mesh['pb'=8,'pa'=32] {'pb'}, dimensions={0}, use_global_device_ids=true | all-gather | bytes 884736 | tf_op jit(solution)/shard_map/all_gather | solution.py:34
  76.7 27.0 %all-gather.2.cloned.1.call-done = bf16[2048,768]{1,0:T(8,128)(2,1)} async-done(((bf16[64,768]{1,0:T(8,128)(2,1)}), bf16[2048,768]{1,0:T(8,128)(2,1)}) %all-gather.2.cloned.1.call-update) | async-done | bytes 3145744 | tf_op jit(solution)/shard_map/all_gather | solution.py:32
  103.7 5.5 fusion
  109.5 1.6 fusion.12
  112.7 6.3 %fusion.29 = f32[512,768]{1,0:T(8,128)} fusion(bf16[2048,768]{1,0:T(8,128)(2,1)} %all-gather.2.cloned.1.call-done, f32[2048,512]{0,1:T(8,128)} %get-tuple-element.25), kind=kOutput, calls=%fused_computation.46 | convolution fusion | flops 1613758464 | bytes 8912896 | tf_op jit(solution)/shard_map/dot_general | solution.py:22
  118.9 237.6 %all-reduce.3.cloned.1.call-done = (f32[16384]{0:T(1024)}, f32[16384]{0:T(1024)}, f32[16384]{0:T(1024)}) async-done(((f32[16384]{0:T(1024)}, f32[16384]{0:T(1024)}, f32[16384]{0:T(1024)}), (f32[16384]{0:T(1024)}, f32[16384]{0:T(1024)}, f32[16384]{0:T(1024)})) %all-reduce.3.cloned.1.call-update) | async-done | bytes 196624 | tf_op jit(solution)/shard_map/psum | solution.py:79
  358.8 5.5 scatter_custom_fusion
  364.4 6.0 %multiply_convert_fusion.2 = bf16[512,768]{1,0:T(8,128)(2,1)S(1)} fusion(f32[512,768]{1,0:T(8,128)} %fusion.29, bf16[2048,768]{1,0:T(8,128)(2,1)} %all-gather.2.cloned.1.call-done, f32[2048]{0:T(1024)S(1)} %dynamic_slice.37, s32[2048]{0:T(1024)S(1)} %iota_add_fusion, s32[512]{0:T(512)S(1)} %iota_add_fusion.1, f32[2048,512]{0,1:T(8,128)} %get-tuple-element.25, ...), kind=kOutput, calls=%fused_computation.33 | convolution fusion | flops 1619525632 | bytes 9719808 | tf_op jit(solution)/shard_map/dot_general | solution.py:22
  370.4 1.3 pad_maximum_fusion
  371.8 4.3 fusion.31
  376.0 2.6 divide_add_fusion
  379.3 2.3 multiply_convert_fusion
  381.6 1.4 dynamic-slice_subtract_fusion
  383.0 32.8 %reduce-scatter.5.cloned.1.call-done = bf16[64,1536]{1,0:T(8,128)(2,1)} async-done(((bf16[512,1536]{1,0:T(8,128)(2,1)}), bf16[64,1536]{1,0:T(8,128)(2,1)}) %reduce-scatter.5.cloned.1.call-update) | async-done | bytes 196624 | tf_op jit(solution)/shard_map/reduce_scatter | solution.py:127
  415.8 1.0 fusion.51
  416.8 126.5 %reduce-scatter.3.cloned.1.call-done = bf16[64,768]{1,0:T(8,128)(2,1)} async-done(((bf16[2048,768]{1,0:T(8,128)(2,1)}), bf16[64,768]{1,0:T(8,128)(2,1)}) %reduce-scatter.3.cloned.1.call-update) | async-done | bytes 98320 | tf_op jit(solution)/shard_map/reduce_scatter | solution.py:117
  543.3 0.9 convert_element_type.46
  544.5 5.0 convolution_convert_fusion
  549.4 1.2 fusion.49
  (38 shorter events, 5.9 us)
Async XLA Ops:
  7.2 96.5 %all-gather.2.cloned.1.call-start = ((), (), s32[]{:S(2)}) async-start(), calls=%async_computation.2 | async-start | bytes 3244032 | tf_op jit(solution)/shard_map/all_gather | solution.py:32
  12.0 0.9 copy-start.1
  13.7 342.9 %all-reduce.3.cloned.1.call-start = ((), (), s32[]{:S(2)}) async-start(), calls=%async_computation.5 | async-start | bytes 393216 | tf_op jit(solution)/shard_map/psum | solution.py:79
  109.5 2.4 copy-start.3
  111.7 0.6 copy-start.4
  112.0 0.6 copy-start.5
  112.6 303.2 %reduce-scatter.5.cloned.1.call-start = ((), (), s32[]{:S(2)}) async-start(), calls=%async_computation.4 | async-start | bytes 1769472 | tf_op jit(solution)/shard_map/reduce_scatter | solution.py:127
  371.7 171.6 %reduce-scatter.3.cloned.1.call-start = ((), (), s32[]{:S(2)}) async-start(), calls=%async_computation.3 | async-start | bytes 3244032 | tf_op jit(solution)/shard_map/reduce_scatter | solution.py:117
  371.8 4.3 copy-start
  381.5 162.7 %copy-start.2 = (f32[192,768]{1,0:T(8,128)S(1)}, f32[192,768]{1,0:T(8,128)}, u32[]{:S(2)}) copy-start(f32[192,768]{1,0:T(8,128)} %copy-done.1) | copy-start | bytes 1769476
Sparse Core Ops, SparseCore 0:
  13.8 89.8 all-gather.1
  112.7 243.7 all-reduce.2
  371.8 43.9 reduce-scatter.4
  419.8 123.4 reduce-scatter.2
where the time goes:
time: 558 us; the launch traced here: 557 us
  waiting for transfers between devices  424 us (76%)
  blocking collectives  60.1 us (11%)
  matrix products  34.4 us (6%)
  other arithmetic  15.8 us (3%)
  between operations  14 us (3%)
  local copies, waits for them, and re-layouts  8.71 us (2%)
    psum x1, waiting for transfers between devices, shards(): lax.psum((lax.dynamic_update_slice(zero_rows, row_part, (row_start,)), la...  238 us
    reduce_scatter x1, waiting for transfers between devices, shards(): lax.psum_scatter((inverse_temp * (plain_sum / row_total[:, None] + mixed_...  127 us
    reduce_scatter x1, waiting for transfers between devices, shards(): lax.psum_scatter(jnp.concatenate([inverse_temp * (plain_sum / column_tota...  32.8 us
    all_gather x1, blocking collectives, shards(): lax.all_gather(unit_low[local_rows:2 * local_rows], 'pb', axis=0, tiled=T...  30.5 us
    all_gather x1, blocking collectives, shards(): lax.all_gather(unit_low[2 * local_rows:], 'pb', axis=0, tiled=True)  29.6 us
    all_gather x1, waiting for transfers between devices, shards(): lax.all_gather(unit_low[:local_rows], 'pa', axis=0, tiled=True)  27 us
    dot_general x2, matrix products, column_product(): lax.dot_general(tile_low, question_block, (((0,), (0,)), ((), ())), prefe...  12.3 us
  transfers between devices with their start and end apart: 4, of which 4 were waited for; matrix products, arithmetic and copies ran while one was open for 4% of the time, Pallas kernels for 0%

commit v1 on v0

v1 whole, which is shorter than its diff:
```python
import jax
import jax.numpy as jnp
from jax import lax
from jax.experimental import pallas as pl
from jax.experimental.pallas import tpu as pltpu
from jax.sharding import PartitionSpec as P

inverse_temp = 40.0
epsilon = 1e-06
f32 = jnp.float32
bf16 = jnp.bfloat16

NZ, NX, NY = 8, 4, 4
ROWS = 64
HALF = 32
GROUP = 1024
WIDTH = 768
MODEL = 4096
CHUNK = 512
TILE = 256


def nt(a, b):
    return lax.dot_general(a, b, (((1,), (1,)), ((), ())), preferred_element_type=f32)


def tn(a, b):
    return lax.dot_general(a, b, (((0,), (0,)), ((), ())), preferred_element_type=f32)


def wide(column, times):
    return jnp.concatenate([column] * times, axis=1)


def kernel(
    xq_ref, xp_ref, xh_ref, idx_ref, w_ref,
    oq_ref, op_ref, oh_ref, lq_ref, lp_ref,
    xs, w, acc, unit, scale, q_all, p_all, h_own, h_all, h_pick, gh_out, gh_in,
    e_s, g_s, tile_s, csum, tq, tp, rcol, crow, hcol, loss_s,
    dq, prt, zl_in, zs_in, dpa, dpb, a1, b1, a2, b2, ge,
    in_sem, w_sem, send, recv, tq_send, tq_recv, tp_send, tp_recv, h_sem, hg_sem, pt_send, pt_recv,
):
    pb, pa = lax.axis_index("pb"), lax.axis_index("pa")
    x, y_lo = pb // 2, pb % 2
    y_hi, z, core = pa // 16, (pa // 2) % 8, pa % 2
    y = y_hi * 2 + y_lo
    d = 1 - 2 * core

    def device(xx, yy, zz, cc):
        return (xx * 2 + yy % 2, (yy // 2) * 16 + zz * 2 + cc)

    def zmod(v):
        return (v + 16) % 8

    def mod4(v):
        return (v + 8) % 4

    q_slot = z * 2 + core
    p_slot = y_hi * 8 + pb

    def q_peer(s):
        return (pb, y_hi * 16 + s)

    def p_peer(s):
        return (s % 8, (s // 8) * 16 + q_slot)

    def slot_of(xx, yy):
        return (yy // 2) * 8 + xx * 2 + yy % 2

    def rows(ref, slot, first=0, count=ROWS):
        return ref.at[pl.ds(pl.multiple_of(slot * ROWS + first, HALF), count)]

    counter = [0]
    started = []

    def remote(src, dst, to):
        n = counter[0]
        counter[0] += 1
        copy = pltpu.make_async_remote_copy(
            src_ref=src, dst_ref=dst, send_sem=send.at[n], recv_sem=recv.at[n],
            device_id=to, device_id_type=pl.DeviceIdType.MESH,
        )
        copy.start()
        started.append(copy)
        return n

    def arrive(n, dst):
        pltpu.make_async_remote_copy(
            src_ref=dst, dst_ref=dst, send_sem=send.at[n], recv_sem=recv.at[n],
            device_id=(pb, pa), device_id_type=pl.DeviceIdType.MESH,
        ).wait_recv()

    inputs = []
    for i, ref in enumerate((xq_ref, xp_ref, xh_ref)):
        copy = pltpu.make_async_copy(ref, xs.at[pl.ds(i * ROWS, ROWS)], in_sem.at[i])
        copy.start()
        inputs.append(copy)
    for k in range(MODEL // CHUNK):
        pltpu.make_async_copy(w_ref.at[pl.ds(k * CHUNK, CHUNK)], w.at[pl.ds(k * CHUNK, CHUNK)], w_sem.at[k]).start()

    barrier = pltpu.get_barrier_semaphore()

    def greet(k, carry):
        pl.semaphore_signal(barrier, inc=1, device_id=q_peer((q_slot + k) % 16), device_id_type=pl.DeviceIdType.MESH)
        pl.semaphore_signal(barrier, inc=1, device_id=p_peer((p_slot + k) % 16), device_id_type=pl.DeviceIdType.MESH)
        return carry

    lax.fori_loop(1, 16, greet, 0)

    for copy in inputs:
        copy.wait()
    acc[...] = jnp.zeros_like(acc)

    def project(k, carry):
        first = pl.multiple_of(k * CHUNK, CHUNK)
        pltpu.make_async_copy(w_ref.at[pl.ds(first, CHUNK)], w.at[pl.ds(first, CHUNK)], w_sem.at[k]).wait()
        acc[...] += jnp.dot(xs[:, pl.ds(first, CHUNK)], w[pl.ds(first, CHUNK), :], preferred_element_type=f32)
        return carry

    lax.fori_loop(0, MODEL // CHUNK, project, 0)

    def normalise(i):
        emb = acc[i * ROWS : (i + 1) * ROWS, :]
        s = lax.rsqrt(jnp.sum(emb * emb, axis=1, keepdims=True) + epsilon)
        u = emb * s
        scale[i * ROWS : (i + 1) * ROWS, :] = jnp.broadcast_to(s, (ROWS, 128))
        unit[i * ROWS : (i + 1) * ROWS, :] = u
        return u.astype(bf16)

    q_all[pl.ds(pl.multiple_of(q_slot * ROWS, ROWS), ROWS), :] = normalise(0)
    p_all[pl.ds(pl.multiple_of(p_slot * ROWS, ROWS), ROWS), :] = normalise(1)
    h_own[...] = normalise(2)
    pl.semaphore_wait(barrier, 30)

    long_to = device(x, y, zmod(z + d), core)
    short_to = device(x, y, zmod(z - d), core)
    other = device(x, y, z, 1 - core)
    xl, xr, yl, yr = mod4(x + d), mod4(x - d), mod4(y + d), mod4(y - d)
    x2, y2 = mod4(x + 2), mod4(y + 2)
    to_xl, to_xr = device(xl, y, z, core), device(xr, y, z, core)
    to_yl, to_yr = device(x, yl, z, core), device(x, yr, z, core)

    def qz(zz, cc):
        return zmod(zz) * 2 + cc

    def push(ref, slot, to, first=0, count=ROWS):
        part = rows(ref, slot, first, count)
        return remote(part, part, to)

    def await_rows(n, ref, slot, first=0, count=ROWS):
        arrive(n, rows(ref, slot, first, count))

    q_long, q_short, q_other, other_slots = [], [], [], []
    for hf in range(2):
        q_long.append(push(q_all, q_slot, long_to, hf * HALF, HALF))
        q_short.append(push(q_all, q_slot, short_to, hf * HALF, HALF))
    p_from_xr = push(p_all, p_slot, to_xl)
    p_from_xl = push(p_all, p_slot, to_xr)
    p_from_yr = push(p_all, p_slot, to_yl)
    p_from_yl = push(p_all, p_slot, to_yr)
    q_other.append(push(q_all, q_slot, other))
    other_slots.append(qz(z, 1 - core))

    keeper = y_hi * 8 + z
    keeper_dev = (keeper // 2, (keeper % 2) * 16 + q_slot)
    is_keeper = z == (2 * pb + y_hi) % 8
    kb = (2 * pb + y_hi) // 8
    ka = core
    sends_hard = jnp.logical_not(jnp.logical_and(is_keeper, kb == y_hi))

    @pl.when(sends_hard)
    def _():
        part = rows(h_all, pb)
        pltpu.make_async_remote_copy(
            src_ref=h_own, dst_ref=part, send_sem=h_sem.at[8], recv_sem=h_sem.at[pb],
            device_id=keeper_dev, device_id_type=pl.DeviceIdType.MESH,
        ).start()

    @pl.when(jnp.logical_not(sends_hard))
    def _():
        h_all[pl.ds(pl.multiple_of(pb * ROWS, ROWS), ROWS), :] = h_own[...]

    def q_wave(step):
        nonlocal q_long, q_short
        nl, ns = [], []
        for hf in range(2):
            slot = qz(z - (step + 1) * d, core)
            await_rows(q_long[hf], q_all, slot, hf * HALF, HALF)
            if step < 3:
                nl.append(push(q_all, slot, long_to, hf * HALF, HALF))
            if step < 3:
                slot2 = qz(z + (step + 1) * d, core)
                await_rows(q_short[hf], q_all, slot2, hf * HALF, HALF)
                if step < 2:
                    ns.append(push(q_all, slot2, short_to, hf * HALF, HALF))
        q_other.append(push(q_all, slot, other))
        other_slots.append(qz(z + (step + 1) * d, 1 - core))
        if step < 3:
            q_other.append(push(q_all, slot2, other))
            other_slots.append(qz(z - (step + 1) * d, 1 - core))
        q_long, q_short = nl, ns

    A, B = 0, HALF
    q_wave(0)
    await_rows(p_from_xr, p_all, slot_of(xr, y))
    n_x2 = push(p_all, slot_of(xr, y), to_xl)
    await_rows(p_from_yr, p_all, slot_of(x, yr))
    n_y2 = push(p_all, slot_of(x, yr), to_yl)
    n_xr_yl = push(p_all, slot_of(xr, y), to_yl, A, HALF)
    n_xr_yr = push(p_all, slot_of(xr, y), to_yr, A, HALF)
    m_yr_xl = push(p_all, slot_of(x, yr), to_xl, B, HALF)
    m_yr_xr = push(p_all, slot_of(x, yr), to_xr, B, HALF)
    await_rows(p_from_xl, p_all, slot_of(xl, y))
    n_xl_yl = push(p_all, slot_of(xl, y), to_yl, A, HALF)
    n_xl_yr = push(p_all, slot_of(xl, y), to_yr, A, HALF)
    await_rows(p_from_yl, p_all, slot_of(x, yl))
    m_yl_xl = push(p_all, slot_of(x, yl), to_xl, B, HALF)
    m_yl_xr = push(p_all, slot_of(x, yl), to_xr, B, HALF)
    q_wave(1)
    await_rows(n_xr_yl, p_all, slot_of(xr, yr), A, HALF)
    k_xr = push(p_all, slot_of(xr, yr), to_yl, A, HALF)
    await_rows(m_yr_xl, p_all, slot_of(xr, yr), B, HALF)
    l_yr = push(p_all, slot_of(xr, yr), to_xl, B, HALF)
    await_rows(n_xl_yl, p_all, slot_of(xl, yr), A, HALF)
    k_xl = push(p_all, slot_of(xl, yr), to_yl, A, HALF)
    await_rows(m_yl_xl, p_all, slot_of(xr, yl), B, HALF)
    l_yl = push(p_all, slot_of(xr, yl), to_xl, B, HALF)
    await_rows(n_x2, p_all, slot_of(x2, y))
    n_x2_yl = push(p_all, slot_of(x2, y), to_yl, A, HALF)
    n_x2_yr = push(p_all, slot_of(x2, y), to_yr, A, HALF)
    await_rows(n_y2, p_all, slot_of(x, y2))
    m_y2_xl = push(p_all, slot_of(x, y2), to_xl, B, HALF)
    m_y2_xr = push(p_all, slot_of(x, y2), to_xr, B, HALF)
    q_wave(2)
    await_rows(n_x2_yl, p_all, slot_of(x2, yr), A, HALF)
    k_x2 = push(p_all, slot_of(x2, yr), to_yl, A, HALF)
    await_rows(m_y2_xl, p_all, slot_of(xr, y2), B, HALF)
    l_y2 = push(p_all, slot_of(xr, y2), to_xl, B, HALF)
    await_rows(n_xr_yr, p_all, slot_of(xr, yl), A, HALF)
    await_rows(n_xl_yr, p_all, slot_of(xl, yl), A, HALF)
    await_rows(m_yr_xr, p_all, slot_of(xl, yr), B, HALF)
    await_rows(m_yl_xr, p_all, slot_of(xl, yl), B, HALF)
    q_wave(3)
    await_rows(n_x2_yr, p_all, slot_of(x2, yl), A, HALF)
    await_rows(m_y2_xr, p_all, slot_of(xl, y2), B, HALF)
    await_rows(k_xr, p_all, slot_of(xr, y2), A, HALF)
    await_rows(k_xl, p_all, slot_of(xl, y2), A, HALF)
    await_rows(l_yr, p_all, slot_of(x2, yr), B, HALF)
    await_rows(l_yl, p_all, slot_of(x2, yl), B, HALF)
    await_rows(k_x2, p_all, slot_of(x2, y2), A, HALF)
    await_rows(l_y2, p_all, slot_of(x2, y2), B, HALF)
    for n, slot in zip(q_other, other_slots):
        await_rows(n, q_all, slot)

    csum[...] = jnp.zeros_like(csum)
    tq[q_slot] = jnp.zeros((16, 128), f32)
    tp[p_slot] = jnp.zeros((16, 128), f32)

    def score(t, carry):
        first = pl.multiple_of(t * TILE, TILE)
        s = nt(q_all[pl.ds(first, TILE), :], p_all[...])
        e = jnp.exp(inverse_temp * s - inverse_temp)
        e_s[pl.ds(first, TILE), :] = e
        csum[...] += jnp.sum(e.reshape(TILE // 8, 8, GROUP), axis=0)
        part = e[:, :128]
        for j in range(1, GROUP // 128):
            part = part + e[:, j * 128 : (j + 1) * 128]
        for j in range(TILE // 128):
            row = jnp.sum(jnp.transpose(part[j * 128 : (j + 1) * 128, :]), axis=0, keepdims=True)
            tq[q_slot, pl.ds(t * (TILE // 128) + j, 1), :] = row
        return carry

    lax.fori_loop(0, GROUP // TILE, score, 0)
    total = jnp.sum(csum[...], axis=0, keepdims=True)
    for j in range(GROUP // 128):
        tp[p_slot, pl.ds(j, 1), :] = total[:, j * 128 : (j + 1) * 128]

    eye = lax.broadcasted_iota(jnp.int32, (128, 128), 0) == lax.broadcasted_iota(jnp.int32, (128, 128), 1)

    def paired(a, b):
        return jnp.sum(jnp.where(eye, inverse_temp * nt(a, b), 0.0), axis=0, keepdims=True)

    @pl.when(is_keeper)
    def _():
        for s in range(8):
            @pl.when(jnp.logical_not(jnp.logical_and(kb == y_hi, pb == s)))
            def _():
                part = h_all.at[pl.ds(s * ROWS, ROWS)]
                pltpu.make_async_remote_copy(
                    src_ref=part, dst_ref=part, send_sem=h_sem.at[8], recv_sem=h_sem.at[s],
                    device_id=(pb, pa), device_id_type=pl.DeviceIdType.MESH,
                ).wait_recv()
        block_base = (kb * 16 + q_slot) * 512
        hidx = idx_ref[y_hi * 2 + ka] - block_base
        for j in range(4):
            hit = lax.broadcasted_iota(jnp.int32, (512, 128), 0) == hidx[j : j + 1, :]
            pick = tn(hit.astype(bf16), h_all[...]).astype(bf16)
            h_pick[j * 128 : (j + 1) * 128, :] = pick
            q_rows = q_all[pl.ds(pl.multiple_of(ka * 512 + j * 128, 128), 128), :]
            p_rows = p_all[pl.ds(pl.multiple_of(kb * 512 + j * 128, 128), 128), :]
            he = jnp.exp(paired(q_rows, pick) - inverse_temp)
            hcol[pl.ds(j, 1), :] = he
            tq[q_slot, pl.ds(ka * 4 + j, 1), :] += he
            diag = paired(q_rows, p_rows)
            tq[q_slot, pl.ds(8 + ka * 4 + j, 1), :] = diag
            tp[p_slot, pl.ds(8 + kb * 4 + j, 1), :] = diag

    def tell(k, carry):
        pltpu.make_async_remote_copy(
            src_ref=tq.at[q_slot], dst_ref=tq.at[q_slot], send_sem=tq_send.at[k], recv_sem=tq_recv.at[q_slot],
            device_id=q_peer((q_slot + k) % 16), device_id_type=pl.DeviceIdType.MESH,
        ).start()
        pltpu.make_async_remote_copy(
            src_ref=tp.at[p_slot], dst_ref=tp.at[p_slot], send_sem=tp_send.at[k], recv_sem=tp_recv.at[p_slot],
            device_id=p_peer((p_slot + k) % 16), device_id_type=pl.DeviceIdType.MESH,
        ).start()
        return carry

    def heard(k, carry):
        sq, sp = (q_slot + k) % 16, (p_slot + k) % 16
        pltpu.make_async_remote_copy(
            src_ref=tq.at[q_slot], dst_ref=tq.at[sq], send_sem=tq_send.at[k], recv_sem=tq_recv.at[sq],
            device_id=(pb, pa), device_id_type=pl.DeviceIdType.MESH,
        ).wait()
        pltpu.make_async_remote_copy(
            src_ref=tp.at[p_slot], dst_ref=tp.at[sp], send_sem=tp_send.at[k], recv_sem=tp_recv.at[sp],
            device_id=(pb, pa), device_id_type=pl.DeviceIdType.MESH,
        ).wait()
        return carry

    lax.fori_loop(1, 16, tell, 0)
    lax.fori_loop(1, 16, heard, 0)
    sq = jnp.sum(tq[...], axis=0)
    sp = jnp.sum(tp[...], axis=0)
    loss_s[0:8, :] = inverse_temp + jnp.log(sq[:8]) - sq[8:]
    loss_s[8:16, :] = inverse_temp + jnp.log(sp[:8]) - sp[8:]
    rinv = inverse_temp / sq[:8]
    cinv = inverse_temp / sp[:8]
    for j in range(8):
        rcol[j * 128 : (j + 1) * 128, :] = jnp.transpose(jnp.broadcast_to(rinv[j : j + 1, :], (128, 128)))
        crow[:, j * 128 : (j + 1) * 128] = jnp.broadcast_to(cinv[j : j + 1, :], (8, 128))
    lrow = loss_s[pl.ds(z, 1), :]
    lq_ref[...] = jnp.where(core == 0, lrow[:, :ROWS], lrow[:, ROWS:])
    lrow = loss_s[pl.ds(8 + y_hi * 4 + x, 1), :]
    lp_ref[...] = jnp.where(y_lo == 0, lrow[:, :ROWS], lrow[:, ROWS:])

    def weigh(t, carry):
        first = pl.multiple_of(t * TILE, TILE)
        factor = wide(rcol[pl.ds(first, TILE), :], GROUP // 128) + crow[0:1, :]
        g_s[pl.ds(first, TILE), :] = (e_s[pl.ds(first, TILE), :] * factor).astype(bf16)
        return carry

    lax.fori_loop(0, GROUP // TILE, weigh, 0)

    @pl.when(is_keeper)
    def _():
        for j in range(4):
            r = pl.multiple_of(ka * 512 + j * 128, 128)
            c = pl.multiple_of(kb * 512 + j * 128, 128)
            factor = rcol[pl.ds(r, 128), :] + crow[0:1, pl.ds(c, 128)]
            value = e_s[pl.ds(r, 128), pl.ds(c, 128)] * factor - jnp.where(eye, 2.0 * inverse_temp, 0.0)
            g_s[pl.ds(r, 128), pl.ds(c, 128)] = value.astype(bf16)
            share = jnp.transpose(jnp.broadcast_to(hcol[j : j + 1, :], (128, 128))) * rcol[pl.ds(r, 128), :]
            gh_in[j * 128 : (j + 1) * 128, :] = wide(share, WIDTH // 128) * q_all[pl.ds(r, 128), :].astype(f32)
            h_pick_f = wide(share, WIDTH // 128) * h_pick[j * 128 : (j + 1) * 128, :].astype(f32)
            tile_s[j * 128 : (j + 1) * 128, :] = h_pick_f
        hidx = idx_ref[y_hi * 2 + ka] - (kb * 16 + q_slot) * 512
        total_h = jnp.zeros((512, WIDTH), f32)
        for j in range(4):
            hit = lax.broadcasted_iota(jnp.int32, (512, 128), 0) == hidx[j : j + 1, :]
            total_h = total_h + jnp.dot(
                hit.astype(bf16), gh_in[j * 128 : (j + 1) * 128, :].astype(bf16), preferred_element_type=f32
            )
        gh_out[0:512, :] = total_h.astype(bf16)
        for s in range(8):
            here = jnp.logical_and(kb == y_hi, pb == s)

            @pl.when(jnp.logical_not(here))
            def _():
                pltpu.make_async_remote_copy(
                    src_ref=gh_out.at[pl.ds(s * ROWS, ROWS)], dst_ref=gh_out.at[pl.ds(512, ROWS)],
                    send_sem=hg_sem.at[s], recv_sem=hg_sem.at[8],
                    device_id=(s, kb * 16 + q_slot), device_id_type=pl.DeviceIdType.MESH,
                ).start()

            @pl.when(here)
            def _():
                gh_out[512 : 512 + ROWS, :] = gh_out[s * ROWS : (s + 1) * ROWS, :]

    t0 = zmod(z + 4) // 2

    def question_tile(i, carry):
        t = (t0 + i) % 4
        first = pl.multiple_of(t * TILE, TILE)
        value = jnp.dot(g_s[pl.ds(first, TILE), :], p_all[...], preferred_element_type=f32)

        @pl.when(jnp.logical_and(is_keeper, t // 2 == ka))
        def _():
            at = pl.multiple_of((t % 2) * TILE, TILE)
            summed = value + tile_s[pl.ds(at, TILE), :]
            for j in range(4):
                dq[j % 2, t * 2 + j // 2] = summed[j * ROWS : (j + 1) * ROWS, :].astype(bf16)

        @pl.when(jnp.logical_not(jnp.logical_and(is_keeper, t // 2 == ka)))
        def _():
            for j in range(4):
                dq[j % 2, t * 2 + j // 2] = value[j * ROWS : (j + 1) * ROWS, :].astype(bf16)

        pltpu.make_async_remote_copy(
            src_ref=dq.at[1 - core, pl.ds(t * 2, 2)], dst_ref=prt.at[pl.ds(t * 2, 2)],
            send_sem=pt_send.at[t], recv_sem=pt_recv.at[t],
            device_id=other, device_id_type=pl.DeviceIdType.MESH,
        ).start()
        return carry

    lax.fori_loop(0, 4, question_tile, 0)

    def passage_tile(t, carry):
        first = pl.multiple_of(t * TILE, TILE)
        value = tn(g_s[:, pl.ds(first, TILE)], q_all[...]).astype(bf16)
        for j in range(4):
            slot = t * 4 + j
            yy = (slot // 8) * 2 + j % 2
            xx = (slot % 8) // 2
            dpa[yy, xx] = value[j * ROWS : j * ROWS + HALF, :]
            dpb[xx, yy] = value[j * ROWS + HALF : (j + 1) * ROWS, :]
        return carry

    lax.fori_loop(0, 4, passage_tile, 0)

    n_a1 = remote(dpa.at[y2], a1.at[0], to_yl)
    n_b1 = remote(dpb.at[x2], b1.at[0], to_xl)
    n_a1s = remote(dpa.at[yr], a1.at[1], to_yr)
    n_b1s = remote(dpb.at[xr], b1.at[1], to_xr)

    def own_sum(k, carry):
        t = k
        pltpu.make_async_remote_copy(
            src_ref=dq.at[1 - core, pl.ds(t * 2, 2)], dst_ref=prt.at[pl.ds(t * 2, 2)],
            send_sem=pt_send.at[t], recv_sem=pt_recv.at[t],
            device_id=other, device_id_type=pl.DeviceIdType.MESH,
        ).wait()
        prt[pl.ds(t * 2, 2)] = (
            prt[pl.ds(t * 2, 2)].astype(f32) + dq[core, pl.ds(t * 2, 2)].astype(f32)
        ).astype(bf16)
        return carry

    lax.fori_loop(0, 4, own_sum, 0)

    def half(ref, hf):
        return ref.at[pl.ds(hf * HALF, HALF)]

    r_long, r_short = [], []
    for hf in range(2):
        r_long.append(remote(half(prt.at[zmod(z + 4)], hf), half(zl_in.at[0], hf), long_to))
        r_short.append(remote(half(prt.at[zmod(z - 3 * d)], hf), half(zs_in.at[0], hf), short_to))

    def q_back(step):
        nonlocal r_long, r_short
        nl, ns = [], []
        for hf in range(2):
            part = slice(hf * HALF, (hf + 1) * HALF)
            arrive(r_long[hf], half(zl_in.at[step], hf))
            if step < 3:
                mine = prt[zmod(z + (3 - step) * d), part, :].astype(f32)
                zl_in[step, part, :] = (zl_in[step, part, :].astype(f32) + mine).astype(bf16)
                nl.append(remote(half(zl_in.at[step], hf), half(zl_in.at[step + 1], hf), long_to))
            if step < 3:
                arrive(r_short[hf], half(zs_in.at[step], hf))
            if step < 2:
                mine = prt[zmod(z - (2 - step) * d), part, :].astype(f32)
                zs_in[step, part, :] = (zs_in[step, part, :].astype(f32) + mine).astype(bf16)
                ns.append(remote(half(zs_in.at[step], hf), half(zs_in.at[step + 1], hf), short_to))
        r_long, r_short = nl, ns

    q_back(0)
    arrive(n_a1, a1.at[0])
    a1[0] = (a1[0].astype(f32) + dpa[yl].astype(f32)).astype(bf16)
    n_a1l = remote(a1.at[0], a1.at[2], to_yl)
    arrive(n_b1, b1.at[0])
    b1[0] = (b1[0].astype(f32) + dpb[xl].astype(f32)).astype(bf16)
    n_b1l = remote(b1.at[0], b1.at[2], to_xl)
    q_back(1)
    arrive(n_a1s, a1.at[1])
    arrive(n_a1l, a1.at[2])
    a1[1] = (a1[1].astype(f32) + a1[2].astype(f32) + dpa[y].astype(f32)).astype(bf16)
    n_a2 = remote(a1.at[1, x2], a2.at[0], to_xl)
    n_a2s = remote(a1.at[1, xr], a2.at[1], to_xr)
    arrive(n_b1s, b1.at[1])
    arrive(n_b1l, b1.at[2])
    b1[1] = (b1[1].astype(f32) + b1[2].astype(f32) + dpb[x].astype(f32)).astype(bf16)
    n_b2 = remote(b1.at[1, y2], b2.at[0], to_yl)
    n_b2s = remote(b1.at[1, yr], b2.at[1], to_yr)
    q_back(2)
    arrive(n_a2, a2.at[0])
    a2[0] = (a2[0].astype(f32) + a1[1, xl].astype(f32)).astype(bf16)
    n_a2l = remote(a2.at[0], a2.at[2], to_xl)
    arrive(n_b2, b2.at[0])
    b2[0] = (b2[0].astype(f32) + b1[1, yl].astype(f32)).astype(bf16)
    n_b2l = remote(b2.at[0], b2.at[2], to_yl)

    def back(grad, i, first, count):
        part = slice(i * ROWS + first, i * ROWS + first + count)
        u = unit[part, :]
        along = jnp.sum(grad * u, axis=1, keepdims=True)
        ge[part, :] = ((grad - u * along) * wide(scale[part, :], WIDTH // 128)).astype(bf16)

    @pl.when(sends_hard)
    def _():
        pltpu.make_async_remote_copy(
            src_ref=gh_out.at[pl.ds(0, ROWS)], dst_ref=gh_out.at[pl.ds(512, ROWS)],
            send_sem=hg_sem.at[0], recv_sem=hg_sem.at[8],
            device_id=(pb, pa), device_id_type=pl.DeviceIdType.MESH,
        ).wait_recv()

    back(gh_out[512 : 512 + ROWS, :].astype(f32), 2, 0, ROWS)

    q_back(3)
    grad_q = prt[z].astype(f32) + zl_in[3].astype(f32) + zs_in[2].astype(f32)
    back(grad_q, 0, 0, ROWS)
    arrive(n_a2s, a2.at[1])
    arrive(n_a2l, a2.at[2])
    back(a2[1].astype(f32) + a2[2].astype(f32) + a1[1, x].astype(f32), 1, 0, HALF)
    arrive(n_b2s, b2.at[1])
    arrive(n_b2l, b2.at[2])
    back(b2[1].astype(f32) + b2[2].astype(f32) + b1[1, y].astype(f32), 1, HALF, HALF)

    def unproject(k, carry):
        first = pl.multiple_of(k * CHUNK, CHUNK)
        value = nt(ge[...], w[pl.ds(first, CHUNK), :]).astype(bf16)
        oq_ref[:, pl.ds(first, CHUNK)] = value[:ROWS]
        op_ref[:, pl.ds(first, CHUNK)] = value[ROWS : 2 * ROWS]
        oh_ref[:, pl.ds(first, CHUNK)] = value[2 * ROWS :]
        return carry

    lax.fori_loop(0, MODEL // CHUNK, unproject, 0)

    for copy in started:
        copy.wait_send()

    @pl.when(sends_hard)
    def _():
        pltpu.make_async_remote_copy(
            src_ref=h_own, dst_ref=rows(h_all, pb), send_sem=h_sem.at[8], recv_sem=h_sem.at[pb],
            device_id=keeper_dev, device_id_type=pl.DeviceIdType.MESH,
        ).wait_send()

    @pl.when(is_keeper)
    def _():
        for s in range(8):
            @pl.when(jnp.logical_not(jnp.logical_and(kb == y_hi, pb == s)))
            def _():
                pltpu.make_async_remote_copy(
                    src_ref=gh_out.at[pl.ds(s * ROWS, ROWS)], dst_ref=gh_out.at[pl.ds(512, ROWS)],
                    send_sem=hg_sem.at[s], recv_sem=hg_sem.at[8],
                    device_id=(s, kb * 16 + q_slot), device_id_type=pl.DeviceIdType.MESH,
                ).wait_send()


COPIES = 110


def shards(questions, passages, hard_rows, hard_index, projection):
    vmem = pl.BlockSpec(memory_space=pltpu.VMEM)
    hbm = pl.BlockSpec(memory_space=pl.ANY)
    out = jax.ShapeDtypeStruct((ROWS, MODEL), bf16)
    loss = jax.ShapeDtypeStruct((1, ROWS), f32)
    V, D = pltpu.VMEM, pltpu.SemaphoreType.DMA
    gq, gp, gh, lq, lp = pl.pallas_call(
        kernel,
        out_shape=(out, out, out, loss, loss),
        in_specs=[hbm, hbm, hbm, vmem, hbm],
        out_specs=(vmem,) * 5,
        scratch_shapes=[
            V((3 * ROWS, MODEL), bf16),
            V((MODEL, WIDTH), bf16),
            V((3 * ROWS, WIDTH), f32),
            V((3 * ROWS, WIDTH), f32),
            V((3 * ROWS, 128), f32),
            V((GROUP, WIDTH), bf16),
            V((GROUP, WIDTH), bf16),
            V((ROWS, WIDTH), bf16),
            V((512, WIDTH), bf16),
            V((512, WIDTH), bf16),
            V((512 + ROWS, WIDTH), bf16),
            V((512, WIDTH), f32),
            V((GROUP, GROUP), f32),
            V((GROUP, GROUP), bf16),
            V((512, WIDTH), f32),
            V((8, GROUP), f32),
            V((16, 16, 128), f32),
            V((16, 16, 128), f32),
            V((GROUP, 128), f32),
            V((8, GROUP), f32),
            V((8, 128), f32),
            V((16, 128), f32),
            V((2, 8, ROWS, WIDTH), bf16),
            V((8, ROWS, WIDTH), bf16),
            V((4, ROWS, WIDTH), bf16),
            V((3, ROWS, WIDTH), bf16),
            V((4, 4, HALF, WIDTH), bf16),
            V((4, 4, HALF, WIDTH), bf16),
            V((3, 4, HALF, WIDTH), bf16),
            V((3, 4, HALF, WIDTH), bf16),
            V((3, HALF, WIDTH), bf16),
            V((3, HALF, WIDTH), bf16),
            V((3 * ROWS, WIDTH), bf16),
            D((3,)), D((MODEL // CHUNK,)),
            D((COPIES,)), D((COPIES,)),
            D((16,)), D((16,)), D((16,)), D((16,)),
            D((9,)), D((9,)), D((4,)), D((4,)),
        ],
        compiler_params=pltpu.CompilerParams(
            collective_id=0, has_side_effects=True, vmem_limit_bytes=56 * 1024 * 1024
        ),
        cost_estimate=pl.CostEstimate(flops=8 * 10**9, bytes_accessed=10**7, transcendentals=10**6),
    )(questions, passages, hard_rows, hard_index.reshape(4, 4, 128), projection)
    return gq, gp, gh, lq.reshape(ROWS), lp.reshape(ROWS)


def solution(mesh):
    in_specs = (P(("pb", "pa"), None), P(("pa", "pb"), None), P(("pa", "pb"), None), P("pb"), P())
    out_specs = (
        P(("pb", "pa"), None),
        P(("pa", "pb"), None),
        P(("pa", "pb"), None),
        P(("pb", "pa")),
        P(("pa", "pb")),
    )
    return jax.shard_map(shards, mesh=mesh, in_specs=in_specs, out_specs=out_specs, check_vma=False)
```

time: 558 us -> 96.8 us (0.17)
  the two profiles are of different devices: /device:TPU:6 before, /device:TPU:36 now
where the time goes in v1:
time: 96.8 us; the launch traced here: 96.5 us
  Pallas kernels  88 us (91%)
  local copies, waits for them, and re-layouts  7.91 us (8%)
    pallas_call x1, Pallas kernels, shards(): pl.pallas_call(kernel, out_shape=(out, out, out, loss, loss), in_specs=[h...  88 us
    unnamed x5, local copies, waits for them, and re-layouts  7.91 us

profile of v1, /device:TPU:36, one launch (start us, length us, event | category | flops | bytes accessed | tf_op | source)
XLA Modules:
  0.0 96.5 jit_solution(12382232692011175202)
XLA Ops:
  0.6 88.0 %shard_map.92 = (bf16[64,4096]{1,0:T(8,128)(2,1)}, bf16[64,4096]{1,0:T(8,128)(2,1)}, bf16[64,4096]{1,0:T(8,128)(2,1)}, f32[1,64]{1,0:T(1,128)}, f32[1,64]{1,0:T(1,128)}) custom-call(bf16[64,4096]{1,0:T(8,128)(2,1)} %xq_ref.1, bf16[64,4096]{1,0:T(8,128)(2,1)} %xp_ref.1, bf16[64,4096]{1,0:T(8,128)(2,1)} %xh_ref.1, s32[4,4,128]{2,1,0:T(4,128)} %bitcast.3, ...), custom_call_target="tpu_custom_call" | custom-call | flops 8000000000 | bytes 10000000 | tf_op jit(solution)/shard_map/pallas_call | solution.py:569
  88.6 1.9 %copy.15 = bf16[64,4096]{1,0:T(8,128)(2,1)} copy(bf16[64,4096]{1,0:T(8,128)(2,1)} %get-tuple-element.20) | data formatting | bytes 1048576
  90.5 1.9 %copy.16 = bf16[64,4096]{1,0:T(8,128)(2,1)} copy(bf16[64,4096]{1,0:T(8,128)(2,1)} %get-tuple-element.21) | data formatting | bytes 1048576
  92.4 1.9 %copy.17 = bf16[64,4096]{1,0:T(8,128)(2,1)} copy(bf16[64,4096]{1,0:T(8,128)(2,1)} %get-tuple-element.22) | data formatting | bytes 1048576
  94.2 1.2 %copy.18 = f32[64]{0:T(128)} copy(f32[64]{0:T(128)} %bitcast.5) | data formatting | bytes 512
  95.4 1.1 %copy.19 = f32[64]{0:T(128)} copy(f32[64]{0:T(128)} %bitcast.4) | data formatting | bytes 512

commit v2 on v1

v2 whole, which is shorter than its diff:
```python
import jax
import jax.numpy as jnp
from jax import lax
from jax.experimental import pallas as pl
from jax.experimental.pallas import tpu as pltpu
from jax.sharding import PartitionSpec as P

inverse_temp = 40.0
epsilon = 1e-06
f32 = jnp.float32
bf16 = jnp.bfloat16

NZ, NX, NY = 8, 4, 4
ROWS = 64
HALF = 32
GROUP = 1024
WIDTH = 768
MODEL = 4096
CHUNK = 1024
TILE = 256


def nt(a, b):
    return lax.dot_general(a, b, (((1,), (1,)), ((), ())), preferred_element_type=f32)


def tn(a, b):
    return lax.dot_general(a, b, (((0,), (0,)), ((), ())), preferred_element_type=f32)


def wide(column, times):
    return jnp.concatenate([column] * times, axis=1)


def kernel(
    xq_ref, xp_ref, xh_ref, idx_ref, w_ref,
    oq_ref, op_ref, oh_ref, lq_ref, lp_ref,
    xs, w, wt, acc, unit, scale, q_all, p_all, h_own, h_rel, h_in, dh_out, dh_rel, dh_in, eh, gh,
    e_s, g_s, tile_s, csum, tq, tp, rcol, crow, rin_s, dg, dgq, dgp, lrow_s,
    dq, prt, zr, zin, dpa, dpb, a1, b1, a2, b2, ge, out_s,
    idx_s, loss_s,
    in_sem, w_sem, send, recv, tq_send, tq_recv, tp_send, tp_recv, dg_send, dg_recv, hop_sem, pt_send, pt_recv, o_sem,
):
    pb, pa = lax.axis_index("pb"), lax.axis_index("pa")
    x, y_lo = pb // 2, pb % 2
    y_hi, z, core = pa // 16, (pa // 2) % 8, pa % 2
    y = y_hi * 2 + y_lo
    d = 1 - 2 * core

    def device(xx, yy, zz, cc):
        return (xx * 2 + yy % 2, (yy // 2) * 16 + zz * 2 + cc)

    def zmod(v):
        return (v + 16) % 8

    def mod4(v):
        return (v + 8) % 4

    q_slot = z * 2 + core
    p_slot = y_hi * 8 + pb

    def q_slot_of(zz):
        return zz * 2 + core

    def q_peer(s):
        return (pb, y_hi * 16 + s)

    def p_peer(s):
        return (s % 8, (s // 8) * 16 + q_slot)

    def slot_of(xx, yy):
        return (yy // 2) * 8 + xx * 2 + yy % 2

    def rows(ref, slot, first=0, count=ROWS):
        return ref.at[pl.ds(pl.multiple_of(slot * ROWS + first, HALF), count)]

    counter = [0]
    started = []

    def remote(src, dst, to):
        n = counter[0]
        counter[0] += 1
        copy = pltpu.make_async_remote_copy(
            src_ref=src, dst_ref=dst, send_sem=send.at[n], recv_sem=recv.at[n],
            device_id=to, device_id_type=pl.DeviceIdType.MESH,
        )
        copy.start()
        started.append(copy)
        return n

    def arrive(n, dst):
        pltpu.make_async_remote_copy(
            src_ref=dst, dst_ref=dst, send_sem=send.at[n], recv_sem=recv.at[n],
            device_id=(pb, pa), device_id_type=pl.DeviceIdType.MESH,
        ).wait_recv()

    inputs = []
    idx_copy = pltpu.make_async_copy(idx_ref, idx_s, in_sem.at[3])
    for i, ref in enumerate((xq_ref, xp_ref, xh_ref)):
        copy = pltpu.make_async_copy(ref, xs.at[pl.ds(i * ROWS, ROWS)], in_sem.at[i])
        copy.start()
        inputs.append(copy)
    for k in range(MODEL // CHUNK):
        pltpu.make_async_copy(w_ref.at[pl.ds(k * CHUNK, CHUNK)], w.at[pl.ds(k * CHUNK, CHUNK)], w_sem.at[k]).start()

    idx_copy.start()

    barrier = pltpu.get_barrier_semaphore()

    def greet(k, carry):
        pl.semaphore_signal(barrier, inc=1, device_id=q_peer((q_slot + k) % 16), device_id_type=pl.DeviceIdType.MESH)
        pl.semaphore_signal(barrier, inc=1, device_id=p_peer((p_slot + k) % 16), device_id_type=pl.DeviceIdType.MESH)
        return carry

    lax.fori_loop(1, 16, greet, 0)

    for copy in inputs:
        copy.wait()
    acc[...] = jnp.zeros_like(acc)

    def project(k, carry):
        first = pl.multiple_of(k * CHUNK, CHUNK)
        pltpu.make_async_copy(w_ref.at[pl.ds(first, CHUNK)], w.at[pl.ds(first, CHUNK)], w_sem.at[k]).wait()
        acc[...] += jnp.dot(xs[:, pl.ds(first, CHUNK)], w[pl.ds(first, CHUNK), :], preferred_element_type=f32)
        return carry

    for k in range(MODEL // CHUNK):
        project(k, 0)

    def normalise(i):
        emb = acc[i * ROWS : (i + 1) * ROWS, :]
        s = lax.rsqrt(jnp.sum(emb * emb, axis=1, keepdims=True) + epsilon)
        u = emb * s
        scale[i * ROWS : (i + 1) * ROWS, :] = jnp.broadcast_to(s, (ROWS, 128))
        unit[i * ROWS : (i + 1) * ROWS, :] = u
        return u.astype(bf16)

    q_all[pl.ds(pl.multiple_of(q_slot * ROWS, ROWS), ROWS), :] = normalise(0)
    p_all[pl.ds(pl.multiple_of(p_slot * ROWS, ROWS), ROWS), :] = normalise(1)
    h_own[...] = normalise(2)
    pl.semaphore_wait(barrier, 30)

    def z_dev(v):
        return device(x, y, zmod(z + v), core)

    other = device(x, y, z, 1 - core)
    xl, xr, yl, yr = mod4(x + d), mod4(x - d), mod4(y + d), mod4(y - d)
    x2, y2 = mod4(x + 2), mod4(y + 2)
    to_xl, to_xr, to_x2 = device(xl, y, z, core), device(xr, y, z, core), device(x2, y, z, core)
    to_yl, to_yr, to_y2 = device(x, yl, z, core), device(x, yr, z, core), device(x, y2, z, core)

    def qz(zz, cc):
        return zmod(zz) * 2 + cc

    def push(ref, slot, to, first=0, count=ROWS):
        part = rows(ref, slot, first, count)
        return remote(part, part, to)

    def await_rows(n, ref, slot, first=0, count=ROWS):
        arrive(n, rows(ref, slot, first, count))

    other_in = []

    def share(v, first=0, count=ROWS):
        n = push(q_all, qz(z + v * d, core), other, first, count)
        other_in.append((n, qz(z - v * d, 1 - core), first, count))

    A, B = 0, HALF
    share(0)
    q2 = [[push(q_all, q_slot, z_dev(2 * d), hf * HALF, HALF), push(q_all, q_slot, z_dev(-2 * d), hf * HALF, HALF)] for hf in range(2)]
    p_from_xr = push(p_all, p_slot, to_xl)
    p_from_xl = push(p_all, p_slot, to_xr)
    p_from_yr = push(p_all, p_slot, to_yl)
    p_from_yl = push(p_all, p_slot, to_yr)
    p_from_x2 = push(p_all, p_slot, to_x2)
    p_from_y2 = push(p_all, p_slot, to_y2)
    q1l = push(q_all, q_slot, z_dev(d))
    q1s = push(q_all, q_slot, z_dev(-d))

    def column(m):
        return m // 2, m % 2

    relay_dev = (pb, y_hi * 16 + zmod(z + d * pb) * 2 + core)
    src_z = zmod(z - d * pb)
    src_dev = (pb, y_hi * 16 + src_z * 2 + core)
    goal_pb, goal_hi = column(y_hi * 8 + src_z)
    goal_dev = (goal_pb, goal_hi * 16 + q_slot)
    mine = 2 * pb + y_hi
    from_hi, from_z = mine // 8, mine % 8
    from_pb = zmod(d * (z - from_z))
    from_dev = (from_pb, from_hi * 16 + q_slot)
    relays_self = pb == 0
    goal_self = jnp.logical_and(goal_pb == pb, goal_hi == y_hi)
    from_self = jnp.logical_and(from_pb == pb, from_hi == y_hi)

    def hop(k, src, dst, to):
        return pltpu.make_async_remote_copy(
            src_ref=src, dst_ref=dst, send_sem=hop_sem.at[2 * k], recv_sem=hop_sem.at[2 * k + 1],
            device_id=to, device_id_type=pl.DeviceIdType.MESH,
        )

    def hop_start(k, src, dst, to, is_self):
        @pl.when(jnp.logical_not(is_self))
        def _():
            hop(k, src, dst, to).start()

        @pl.when(is_self)
        def _():
            dst[...] = src[...]

    def hop_recv(k, src, dst, to, is_self):
        @pl.when(jnp.logical_not(is_self))
        def _():
            hop(k, src, dst, to).wait_recv()

    def hop_sent(k, src, dst, to, is_self):
        @pl.when(jnp.logical_not(is_self))
        def _():
            hop(k, src, dst, to).wait_send()

    h1 = (0, h_own, h_rel, relay_dev, relays_self)
    h2 = (1, h_rel, h_in, goal_dev, goal_self)
    h3 = (2, dh_out, dh_rel, from_dev, from_self)
    h4 = (3, dh_rel, dh_in, src_dev, relays_self)

    await_rows(p_from_xr, p_all, slot_of(xr, y))
    n_xr_yl = push(p_all, slot_of(xr, y), to_yl, A, HALF)
    n_xr_yr = push(p_all, slot_of(xr, y), to_yr, A, HALF)
    await_rows(p_from_yr, p_all, slot_of(x, yr))
    m_yr_xl = push(p_all, slot_of(x, yr), to_xl, B, HALF)
    m_yr_xr = push(p_all, slot_of(x, yr), to_xr, B, HALF)
    await_rows(p_from_xl, p_all, slot_of(xl, y))
    n_xl_yl = push(p_all, slot_of(xl, y), to_yl, A, HALF)
    n_xl_yr = push(p_all, slot_of(xl, y), to_yr, A, HALF)
    await_rows(p_from_yl, p_all, slot_of(x, yl))
    m_yl_xl = push(p_all, slot_of(x, yl), to_xl, B, HALF)
    m_yl_xr = push(p_all, slot_of(x, yl), to_xr, B, HALF)
    q4, q3l, q3s = [], [], []
    for hf in range(2):
        f = hf * HALF
        await_rows(q2[hf][0], q_all, qz(z - 2 * d, core), f, HALF)
        share(-2, f, HALF)
        q4.append(push(q_all, qz(z - 2 * d, core), z_dev(2 * d), f, HALF))
        q3l.append(push(q_all, qz(z - 2 * d, core), z_dev(d), f, HALF))
        await_rows(q2[hf][1], q_all, qz(z + 2 * d, core), f, HALF)
        share(2, f, HALF)
        q3s.append(push(q_all, qz(z + 2 * d, core), z_dev(-d), f, HALF))
    hop_start(*h1)
    await_rows(q1l, q_all, qz(z - d, core))
    share(-1)
    await_rows(q1s, q_all, qz(z + d, core))
    share(1)
    await_rows(p_from_x2, p_all, slot_of(x2, y))
    n_x2_y2 = push(p_all, slot_of(x2, y), to_y2, A, HALF)
    n_x2_yl = push(p_all, slot_of(x2, y), to_yl, A, HALF)
    n_x2_yr = push(p_all, slot_of(x2, y), to_yr, A, HALF)
    await_rows(p_from_y2, p_all, slot_of(x, y2))
    m_y2_x2 = push(p_all, slot_of(x, y2), to_x2, B, HALF)
    m_y2_xl = push(p_all, slot_of(x, y2), to_xl, B, HALF)
    m_y2_xr = push(p_all, slot_of(x, y2), to_xr, B, HALF)
    await_rows(n_xr_yl, p_all, slot_of(xr, yr), A, HALF)
    k_xr = push(p_all, slot_of(xr, yr), to_yl, A, HALF)
    await_rows(m_yr_xl, p_all, slot_of(xr, yr), B, HALF)
    l_yr = push(p_all, slot_of(xr, yr), to_xl, B, HALF)
    await_rows(n_xl_yl, p_all, slot_of(xl, yr), A, HALF)
    k_xl = push(p_all, slot_of(xl, yr), to_yl, A, HALF)
    await_rows(m_yl_xl, p_all, slot_of(xr, yl), B, HALF)
    l_yl = push(p_all, slot_of(xr, yl), to_xl, B, HALF)
    for hf in range(2):
        f = hf * HALF
        await_rows(q3s[hf], q_all, qz(z + 3 * d, core), f, HALF)
        share(3, f, HALF)
        await_rows(q3l[hf], q_all, qz(z - 3 * d, core), f, HALF)
        share(-3, f, HALF)
    for hf in range(2):
        f = hf * HALF
        await_rows(q4[hf], q_all, qz(z + 4, core), f, HALF)
        share(4, f, HALF)
    await_rows(n_xr_yr, p_all, slot_of(xr, yl), A, HALF)
    await_rows(n_xl_yr, p_all, slot_of(xl, yl), A, HALF)
    await_rows(m_yr_xr, p_all, slot_of(xl, yr), B, HALF)
    await_rows(m_yl_xr, p_all, slot_of(xl, yl), B, HALF)
    await_rows(n_x2_y2, p_all, slot_of(x2, y2), A, HALF)
    await_rows(m_y2_x2, p_all, slot_of(x2, y2), B, HALF)
    await_rows(n_x2_yl, p_all, slot_of(x2, yr), A, HALF)
    await_rows(m_y2_xl, p_all, slot_of(xr, y2), B, HALF)
    await_rows(n_x2_yr, p_all, slot_of(x2, yl), A, HALF)
    await_rows(m_y2_xr, p_all, slot_of(xl, y2), B, HALF)
    await_rows(k_xr, p_all, slot_of(xr, y2), A, HALF)
    await_rows(k_xl, p_all, slot_of(xl, y2), A, HALF)
    await_rows(l_yr, p_all, slot_of(x2, yr), B, HALF)
    await_rows(l_yl, p_all, slot_of(x2, yl), B, HALF)
    for n, slot, first, count in other_in:
        await_rows(n, q_all, slot, first, count)

    hop_recv(*h1)
    hop_start(*h2)

    csum[...] = jnp.zeros_like(csum)

    def score(t, carry):
        first = pl.multiple_of(t * TILE, TILE)
        s = nt(q_all[pl.ds(first, TILE), :], p_all[...])
        e = jnp.exp(inverse_temp * s - inverse_temp)
        e_s[pl.ds(first, TILE), :] = e
        csum[...] += jnp.sum(e.reshape(TILE // 8, 8, GROUP), axis=0)
        part = e[:, :128]
        for j in range(1, GROUP // 128):
            part = part + e[:, j * 128 : (j + 1) * 128]
        for j in range(TILE // 128):
            row = jnp.sum(jnp.transpose(part[j * 128 : (j + 1) * 128, :]), axis=0, keepdims=True)
            tq[q_slot, pl.ds(t * (TILE // 128) + j, 1), :] = row
        return carry

    for t in range(GROUP // TILE):
        score(t, 0)
    total = jnp.sum(csum[...], axis=0, keepdims=True)
    for j in range(GROUP // 128):
        tp[p_slot, pl.ds(j, 1), :] = total[:, j * 128 : (j + 1) * 128]

    hop_recv(*h2)
    q_half = pl.ds(pl.multiple_of(core * 512, 512), 512)
    idx_copy.wait()
    hidx = idx_s[y_hi * 2 + core] - (from_hi * 16 + q_slot_of(from_z)) * 512 - from_pb * ROWS
    hidx = jnp.concatenate([hidx[j : j + 1, :] for j in range(4)], axis=1)
    named = lax.broadcasted_iota(jnp.int32, (ROWS, 512), 0) == hidx
    e_hard = jnp.exp(inverse_temp * nt(h_in[...], q_all[q_half, :]) - inverse_temp)
    e_hard = jnp.where(named, e_hard, 0.0)
    eh[...] = e_hard
    hard_sum = jnp.sum(e_hard, axis=0, keepdims=True)
    for j in range(4):
        tq[q_slot, pl.ds(core * 4 + j, 1), :] += hard_sum[:, j * 128 : (j + 1) * 128]

    eye = lax.broadcasted_iota(jnp.int32, (128, 128), 0) == lax.broadcasted_iota(jnp.int32, (128, 128), 1)

    def tell(k, carry):
        pltpu.make_async_remote_copy(
            src_ref=tq.at[q_slot], dst_ref=tq.at[q_slot], send_sem=tq_send.at[k], recv_sem=tq_recv.at[q_slot],
            device_id=q_peer((q_slot + k) % 16), device_id_type=pl.DeviceIdType.MESH,
        ).start()
        pltpu.make_async_remote_copy(
            src_ref=tp.at[p_slot], dst_ref=tp.at[p_slot], send_sem=tp_send.at[k], recv_sem=tp_recv.at[p_slot],
            device_id=p_peer((p_slot + k) % 16), device_id_type=pl.DeviceIdType.MESH,
        ).start()
        return carry

    def heard(k, carry):
        sq, sp = (q_slot + k) % 16, (p_slot + k) % 16
        pltpu.make_async_remote_copy(
            src_ref=tq.at[q_slot], dst_ref=tq.at[sq], send_sem=tq_send.at[k], recv_sem=tq_recv.at[sq],
            device_id=(pb, pa), device_id_type=pl.DeviceIdType.MESH,
        ).wait()
        pltpu.make_async_remote_copy(
            src_ref=tp.at[p_slot], dst_ref=tp.at[sp], send_sem=tp_send.at[k], recv_sem=tp_recv.at[sp],
            device_id=(pb, pa), device_id_type=pl.DeviceIdType.MESH,
        ).wait()
        return carry

    for k in range(1, 16):
        tell(k, 0)

    is_keeper = z == mine % 8
    kb = mine // 8
    ka = core

    @pl.when(is_keeper)
    def _():
        for j in range(4):
            q_rows = q_all[pl.ds(pl.multiple_of(ka * 512 + j * 128, 128), 128), :]
            p_rows = p_all[pl.ds(pl.multiple_of(kb * 512 + j * 128, 128), 128), :]
            diag = jnp.where(eye, inverse_temp * nt(q_rows, p_rows), 0.0)
            dg[j : j + 1, :] = jnp.sum(diag, axis=0, keepdims=True)

    def diag_copy(k, dst, to, at):
        return pltpu.make_async_remote_copy(
            src_ref=dg, dst_ref=dst, send_sem=dg_send.at[k], recv_sem=dg_recv.at[at],
            device_id=to, device_id_type=pl.DeviceIdType.MESH,
        )

    def keep(act):
        @pl.when(is_keeper)
        def _():
            for k in range(8):
                sq, sp = ka * 8 + k, kb * 8 + k

                @pl.when(sq != q_slot)
                def _():
                    act(diag_copy(k, dgq, q_peer(sq), 0))

                @pl.when(sp != p_slot)
                def _():
                    act(diag_copy(8 + k, dgp, p_peer(sp), 1))

    keep(lambda copy: copy.start())
    dgq_self = jnp.logical_and(is_keeper, q_slot // 8 == ka)
    dgp_self = jnp.logical_and(is_keeper, p_slot // 8 == kb)

    @pl.when(dgq_self)
    def _():
        dgq[...] = dg[...]

    @pl.when(dgp_self)
    def _():
        dgp[...] = dg[...]

    def turn(k, carry):
        first = pl.multiple_of(k * CHUNK, CHUNK)
        wt[:, pl.ds(first, CHUNK)] = jnp.transpose(w[pl.ds(first, CHUNK), :])
        return carry

    lax.fori_loop(0, MODEL // CHUNK, turn, 0)
    for k in range(1, 16):
        heard(k, 0)
    sq = jnp.sum(tq[...], axis=0)
    sp = jnp.sum(tp[...], axis=0)
    rinv = inverse_temp / sq
    cinv = inverse_temp / sp
    rin_s[...] = rinv
    lrow_s[0:8, :] = sq
    lrow_s[8:16, :] = sp

    hard_weight = jnp.concatenate([rin_s[pl.ds(core * 4 + j, 1), :] for j in range(4)], axis=1)
    gh[...] = (eh[...] * hard_weight).astype(bf16)
    dh_out[...] = jnp.dot(gh[...], q_all[q_half, :], preferred_element_type=f32).astype(bf16)
    hop_start(*h3)
    for j in range(8):
        rcol[j * 128 : (j + 1) * 128, :] = jnp.transpose(jnp.broadcast_to(rinv[j : j + 1, :], (128, 128)))
        crow[:, j * 128 : (j + 1) * 128] = jnp.broadcast_to(cinv[j : j + 1, :], (8, 128))
    tile_s[...] = tn(gh[...], h_in[...])

    @pl.when(is_keeper)
    def _():
        for j in range(4):
            r = pl.multiple_of(ka * 512 + j * 128, 128)
            c = pl.multiple_of(kb * 512 + j * 128, 128)
            factor = rcol[pl.ds(r, 128), :] + crow[0:1, pl.ds(c, 128)]
            e_s[pl.ds(r, 128), pl.ds(c, 128)] -= jnp.where(eye, 2.0 * inverse_temp / factor, 0.0)

    t0 = zmod(z + 4) // 2

    def question_tile(i, carry):
        t = (t0 + i) % 4
        first = pl.multiple_of(t * TILE, TILE)
        factor = wide(rcol[pl.ds(first, TILE), :], GROUP // 128) + crow[0:1, :]
        weights = (e_s[pl.ds(first, TILE), :] * factor).astype(bf16)
        g_s[pl.ds(first, TILE), :] = weights
        value = jnp.dot(weights, p_all[...], preferred_element_type=f32)
        here = (t // 2 == core).astype(f32)
        value = value + here * tile_s[pl.ds(pl.multiple_of((t % 2) * TILE, TILE), TILE), :]
        for j in range(4):
            dq[j % 2, t * 2 + j // 2] = value[j * ROWS : (j + 1) * ROWS, :].astype(bf16)
        pltpu.make_async_remote_copy(
            src_ref=dq.at[1 - core, pl.ds(t * 2, 2)], dst_ref=prt.at[pl.ds(t * 2, 2)],
            send_sem=pt_send.at[t], recv_sem=pt_recv.at[t],
            device_id=other, device_id_type=pl.DeviceIdType.MESH,
        ).start()
        return carry

    for i in range(4):
        question_tile(i, 0)

    def passage_tile(t, carry):
        first = pl.multiple_of(t * TILE, TILE)
        value = tn(g_s[:, pl.ds(first, TILE)], q_all[...]).astype(bf16)
        for j in range(4):
            slot = t * 4 + j
            yy = (slot // 8) * 2 + j % 2
            xx = (slot % 8) // 2
            dpa[yy, xx] = value[j * ROWS : j * ROWS + HALF, :]
            dpb[xx, yy] = value[j * ROWS + HALF : (j + 1) * ROWS, :]
        return carry

    for t in range(2):
        passage_tile(t, 0)

    def own_sum(k, carry):
        t = k
        pltpu.make_async_remote_copy(
            src_ref=dq.at[1 - core, pl.ds(t * 2, 2)], dst_ref=prt.at[pl.ds(t * 2, 2)],
            send_sem=pt_send.at[t], recv_sem=pt_recv.at[t],
            device_id=other, device_id_type=pl.DeviceIdType.MESH,
        ).wait()
        prt[pl.ds(t * 2, 2)] = (
            prt[pl.ds(t * 2, 2)].astype(f32) + dq[core, pl.ds(t * 2, 2)].astype(f32)
        ).astype(bf16)
        return carry

    for i in range(4):
        own_sum((t0 + i) % 4, 0)

    def half(ref, hf):
        return ref.at[pl.ds(hf * HALF, HALF)]

    r4, r3l, r3s = [], [], []
    for hf in range(2):
        r4.append(remote(half(prt.at[zmod(z + 4)], hf), half(zr.at[0], hf), z_dev(-2 * d)))
        r3l.append(remote(half(prt.at[zmod(z - 3 * d)], hf), half(zr.at[1], hf), z_dev(-d)))
        r3s.append(remote(half(prt.at[zmod(z + 3 * d)], hf), half(zr.at[2], hf), z_dev(d)))
    r1l = remote(prt.at[zmod(z - d)], zin.at[0], z_dev(-d))
    r1s = remote(prt.at[zmod(z + d)], zin.at[1], z_dev(d))

    for t in range(2, 4):
        passage_tile(t, 0)

    def pair(ref, i):
        return ref.at[pl.ds(i * 2, 2)]

    n_a1 = [remote(pair(dpa.at[y2], i), pair(a1.at[0], i), to_yr) for i in range(2)]
    n_b1 = [remote(pair(dpb.at[x2], i), pair(b1.at[0], i), to_xr) for i in range(2)]
    n_a1s = remote(dpa.at[yl], a1.at[1], to_yl)
    n_b1s = remote(dpb.at[xl], b1.at[1], to_xl)

    n_a1l, n_b1l = [], []
    for i in range(2):
        two = slice(i * 2, i * 2 + 2)
        arrive(n_a1[i], pair(a1.at[0], i))
        a1[0, two] = (a1[0, two].astype(f32) + dpa[yr, two].astype(f32)).astype(bf16)
        n_a1l.append(remote(pair(a1.at[0], i), pair(a1.at[2], i), to_yr))
        arrive(n_b1[i], pair(b1.at[0], i))
        b1[0, two] = (b1[0, two].astype(f32) + dpb[xr, two].astype(f32)).astype(bf16)
        n_b1l.append(remote(pair(b1.at[0], i), pair(b1.at[2], i), to_xr))

    r2l, r2s = [], []
    for hf in range(2):
        part = slice(hf * HALF, (hf + 1) * HALF)
        arrive(r3s[hf], half(zr.at[2], hf))
        zr[2, part, :] = (zr[2, part, :].astype(f32) + prt[zmod(z + 2 * d), part, :].astype(f32)).astype(bf16)
        r2s.append(remote(half(zr.at[2], hf), half(zin.at[3], hf), z_dev(2 * d)))
        arrive(r3l[hf], half(zr.at[1], hf))
        arrive(r4[hf], half(zr.at[0], hf))
        zr[1, part, :] = (
            zr[1, part, :].astype(f32) + zr[0, part, :].astype(f32) + prt[zmod(z - 2 * d), part, :].astype(f32)
        ).astype(bf16)
        r2l.append(remote(half(zr.at[1], hf), half(zin.at[2], hf), z_dev(-2 * d)))

    hop_recv(*h3)
    hop_start(*h4)

    arrive(n_a1s, a1.at[1])
    for i in range(2):
        arrive(n_a1l[i], pair(a1.at[2], i))
    a1[1] = (a1[1].astype(f32) + a1[2].astype(f32) + dpa[y].astype(f32)).astype(bf16)
    n_a2 = [remote(a1.at[1, xx], a2.at[i], to) for i, (xx, to) in enumerate(((x2, to_x2), (xl, to_xl), (xr, to_xr)))]
    arrive(n_b1s, b1.at[1])
    for i in range(2):
        arrive(n_b1l[i], pair(b1.at[2], i))
    b1[1] = (b1[1].astype(f32) + b1[2].astype(f32) + dpb[x].astype(f32)).astype(bf16)
    n_b2 = [remote(b1.at[1, yy], b2.at[i], to) for i, (yy, to) in enumerate(((y2, to_y2), (yl, to_yl), (yr, to_yr)))]

    def back(grad, i, first, count):
        part = slice(i * ROWS + first, i * ROWS + first + count)
        u = unit[part, :]
        along = jnp.sum(grad * u, axis=1, keepdims=True)
        ge[part, :] = ((grad - u * along) * wide(scale[part, :], WIDTH // 128)).astype(bf16)

    keeper_q = mine % 8
    group_p = y_hi * 8 + z

    @pl.when(jnp.logical_not(dgq_self))
    def _():
        diag_copy(0, dgq, (pb, y_hi * 16 + keeper_q * 2 + z // 4), 0).wait_recv()

    @pl.when(jnp.logical_not(dgp_self))
    def _():
        diag_copy(0, dgp, (group_p // 2, (group_p % 2) * 16 + q_slot), 1).wait_recv()

    def loss(total_row, diag, first):
        value = inverse_temp + jnp.log(total_row) - diag
        return jnp.where(first, value[:, :ROWS], value[:, ROWS:])

    loss_s[0, 0:1, 0:ROWS] = loss(lrow_s[pl.ds(z, 1), :], dgq[pl.ds(z % 4, 1), :], core == 0)
    loss_s[1, 0:1, 0:ROWS] = loss(lrow_s[pl.ds(8 + y_hi * 4 + x, 1), :], dgp[pl.ds(x, 1), :], y_lo == 0)
    loss_copies = [pltpu.make_async_copy(loss_s.at[i], ref, o_sem.at[3, i]) for i, ref in enumerate((lq_ref, lp_ref))]
    for copy in loss_copies:
        copy.start()

    hop_recv(*h4)
    back(dh_in[...].astype(f32), 2, 0, ROWS)

    arrive(r1l, zin.at[0])
    arrive(r1s, zin.at[1])
    for hf in range(2):
        arrive(r2s[hf], half(zin.at[3], hf))
        arrive(r2l[hf], half(zin.at[2], hf))
    back(jnp.sum(zin[...].astype(f32), axis=0) + prt[z].astype(f32), 0, 0, ROWS)
    for i in range(3):
        arrive(n_a2[i], a2.at[i])
    back(jnp.sum(a2[...].astype(f32), axis=0) + a1[1, x].astype(f32), 1, 0, HALF)
    for i in range(3):
        arrive(n_b2[i], b2.at[i])
    back(jnp.sum(b2[...].astype(f32), axis=0) + b1[1, y].astype(f32), 1, HALF, HALF)

    def out_copies(k):
        columns = pl.ds(pl.multiple_of(k * CHUNK, CHUNK), CHUNK)
        return [
            pltpu.make_async_copy(out_s.at[pl.ds(i * ROWS, ROWS), columns], ref.at[:, columns], o_sem.at[i, k])
            for i, ref in enumerate((oq_ref, op_ref, oh_ref))
        ]

    def unproject(k, carry):
        first = pl.multiple_of(k * CHUNK, CHUNK)
        out_s[:, pl.ds(first, CHUNK)] = jnp.dot(
            ge[...], wt[:, pl.ds(first, CHUNK)], preferred_element_type=f32
        ).astype(bf16)
        for copy in out_copies(k):
            copy.start()
        return carry

    for k in range(MODEL // CHUNK):
        unproject(k, 0)

    for copy in started:
        copy.wait_send()
    for h in (h1, h2, h3, h4):
        hop_sent(*h)
    keep(lambda copy: copy.wait_send())
    for k in range(MODEL // CHUNK):
        for copy in out_copies(k):
            copy.wait()
    for copy in loss_copies:
        copy.wait()


def hand_on(gq, gp, gh, lq, lp, oq, op, oh, olq, olp, stage, lstage, lflat, in_sem, out_sem):
    arrivals = [pltpu.make_async_copy(src, stage.at[i], in_sem.at[i]) for i, src in enumerate((gq, gp, gh))]
    losses = [pltpu.make_async_copy(src, lstage.at[i], in_sem.at[3 + i]) for i, src in enumerate((lq, lp))]
    leaving = [pltpu.make_async_copy(stage.at[i], dst, out_sem.at[i]) for i, dst in enumerate((oq, op, oh))]
    leaving += [pltpu.make_async_copy(lflat.at[i], dst, out_sem.at[3 + i]) for i, dst in enumerate((olq, olp))]
    for copy in losses + arrivals:
        copy.start()
    for i, copy in enumerate(losses):
        copy.wait()
        lflat[i, :] = lstage[i, 0, 0:ROWS]
        leaving[3 + i].start()
    for i, copy in enumerate(arrivals):
        copy.wait()
        leaving[i].start()
    for copy in leaving:
        copy.wait()


COPIES = 120


def shards(questions, passages, hard_rows, hard_index, projection):
    vmem = pl.BlockSpec(memory_space=pltpu.VMEM)
    hbm = pl.BlockSpec(memory_space=pl.ANY)
    out = jax.ShapeDtypeStruct((ROWS, MODEL), bf16)
    loss = jax.ShapeDtypeStruct((8, 128), f32)
    flat = jax.ShapeDtypeStruct((ROWS,), f32)
    V, D = pltpu.VMEM, pltpu.SemaphoreType.DMA
    gq, gp, gh, lq, lp = pl.pallas_call(
        kernel,
        out_shape=(out, out, out, loss, loss),
        in_specs=[hbm] * 5,
        out_specs=(hbm,) * 5,
        scratch_shapes=[
            V((3 * ROWS, MODEL), bf16),
            V((MODEL, WIDTH), bf16),
            V((WIDTH, MODEL), bf16),
            V((3 * ROWS, WIDTH), f32),
            V((3 * ROWS, WIDTH), f32),
            V((3 * ROWS, 128), f32),
            V((GROUP, WIDTH), bf16),
            V((GROUP, WIDTH), bf16),
            V((ROWS, WIDTH), bf16),
            V((ROWS, WIDTH), bf16),
            V((ROWS, WIDTH), bf16),
            V((ROWS, WIDTH), bf16),
            V((ROWS, WIDTH), bf16),
            V((ROWS, WIDTH), bf16),
            V((ROWS, 512), f32),
            V((ROWS, 512), bf16),
            V((GROUP, GROUP), f32),
            V((GROUP, GROUP), bf16),
            V((512, WIDTH), f32),
            V((8, GROUP), f32),
            V((16, 8, 128), f32),
            V((16, 8, 128), f32),
            V((GROUP, 128), f32),
            V((8, GROUP), f32),
            V((8, 128), f32),
            V((8, 128), f32),
            V((8, 128), f32),
            V((8, 128), f32),
            V((16, 128), f32),
            V((2, 8, ROWS, WIDTH), bf16),
            V((8, ROWS, WIDTH), bf16),
            V((3, ROWS, WIDTH), bf16),
            V((4, ROWS, WIDTH), bf16),
            V((4, 4, HALF, WIDTH), bf16),
            V((4, 4, HALF, WIDTH), bf16),
            V((3, 4, HALF, WIDTH), bf16),
            V((3, 4, HALF, WIDTH), bf16),
            V((3, HALF, WIDTH), bf16),
            V((3, HALF, WIDTH), bf16),
            V((3 * ROWS, WIDTH), bf16),
            V((3 * ROWS, MODEL), bf16),
            V((4, 4, 128), jnp.int32),
            V((2, 8, 128), f32),
            D((4,)), D((MODEL // CHUNK,)),
            D((COPIES,)), D((COPIES,)),
            D((16,)), D((16,)), D((16,)), D((16,)),
            D((16,)), D((2,)), D((8,)), D((4,)), D((4,)), D((4, MODEL // CHUNK)),
        ],
        compiler_params=pltpu.CompilerParams(
            collective_id=0, has_side_effects=True, vmem_limit_bytes=56 * 1024 * 1024
        ),
        cost_estimate=pl.CostEstimate(flops=8 * 10**9, bytes_accessed=10**7, transcendentals=10**6),
    )(questions, passages, hard_rows, hard_index.reshape(4, 4, 128), projection)
    return pl.pallas_call(
        hand_on,
        out_shape=(out, out, out, flat, flat),
        in_specs=(hbm,) * 5,
        out_specs=(hbm,) * 5,
        scratch_shapes=[V((3, ROWS, MODEL), bf16), V((2, 8, 128), f32), V((2, ROWS), f32), D((5,)), D((5,))],
        compiler_params=pltpu.CompilerParams(vmem_limit_bytes=56 * 1024 * 1024),
        cost_estimate=pl.CostEstimate(flops=0, bytes_accessed=3 * 10**6, transcendentals=0),
    )(gq, gp, gh, lq, lp)


def solution(mesh):
    in_specs = (P(("pb", "pa"), None), P(("pa", "pb"), None), P(("pa", "pb"), None), P("pb"), P())
    out_specs = (
        P(("pb", "pa"), None),
        P(("pa", "pb"), None),
        P(("pa", "pb"), None),
        P(("pb", "pa")),
        P(("pa", "pb")),
    )
    return jax.shard_map(shards, mesh=mesh, in_specs=in_specs, out_specs=out_specs, check_vma=False)
```

time: 96.8 us -> 69.7 us (0.72)
  Pallas kernels: 88 us -> 68.8 us
  local copies, waits for them, and re-layouts: 7.91 us -> 0 us
    pallas_call x1, Pallas kernels: 88 us -> 66.5 us  [shards(): pl.pallas_call(kernel, out_shape=(out, out, out, loss, loss), in_specs=[h...]
    unnamed x5 -> x0, local copies, waits for them, and re-layouts: 7.91 us -> none
    pallas_call x0 -> x1, Pallas kernels: none -> 2.28 us  [shards(): pl.pallas_call(hand_on, out_shape=(out, out, out, flat, flat), in_specs=(...]
where the time goes in v2:
time: 69.7 us; the launch traced here: 69.6 us
  Pallas kernels  68.8 us (99%)
  between operations  0.8 us (1%)
    pallas_call x1, Pallas kernels, shards(): pl.pallas_call(kernel, out_shape=(out, out, out, loss, loss), in_specs=[h...  66.5 us
    pallas_call x1, Pallas kernels, shards(): pl.pallas_call(hand_on, out_shape=(out, out, out, flat, flat), in_specs=(...  2.28 us

profile of v2, /device:TPU:36, one launch (start us, length us, event | category | flops | bytes accessed | tf_op | source)
XLA Modules:
  0.0 69.6 jit_solution(15525303762779318344)
XLA Ops:
  0.6 66.5 %shard_map.92 = (bf16[64,4096]{1,0:T(8,128)(2,1)}, bf16[64,4096]{1,0:T(8,128)(2,1)}, bf16[64,4096]{1,0:T(8,128)(2,1)}, f32[8,128]{1,0:T(8,128)}, f32[8,128]{1,0:T(8,128)}) custom-call(bf16[64,4096]{1,0:T(8,128)(2,1)} %xq_ref.1, bf16[64,4096]{1,0:T(8,128)(2,1)} %xp_ref.1, bf16[64,4096]{1,0:T(8,128)(2,1)} %xh_ref.1, s32[4,4,128]{2,1,0:T(4,128)} %bitcast.1, ...), custom_call_target="tpu_custom_call" | custom-call | flops 8000000000 | bytes 10000000 | tf_op jit(solution)/shard_map/pallas_call | solution.py:652
  67.2 2.3 %shard_map.93 = (bf16[64,4096]{1,0:T(8,128)(2,1)}, bf16[64,4096]{1,0:T(8,128)(2,1)}, bf16[64,4096]{1,0:T(8,128)(2,1)}, f32[64]{0:T(128)}, f32[64]{0:T(128)}) custom-call(bf16[64,4096]{1,0:T(8,128)(2,1)} %get-tuple-element.10.gq, bf16[64,4096]{1,0:T(8,128)(2,1)} %get-tuple-element.11.gp, bf16[64,4096]{1,0:T(8,128)(2,1)} %get-tuple-element.12.gh, ...), custom_call_target="tpu_custom_call" | custom-call | bytes 3000000 | tf_op jit(solution)/shard_map/pallas_call | solution.py:711

commit v3 on v2

--- a/solution.py
+++ b/solution.py
@@ -1,3 +1,5 @@
+import math
+
 import jax
 import jax.numpy as jnp
 from jax import lax
@@ -35,11 +37,11 @@
 def kernel(
     xq_ref, xp_ref, xh_ref, idx_ref, w_ref,
     oq_ref, op_ref, oh_ref, lq_ref, lp_ref,
-    xs, w, wt, acc, unit, scale, q_all, p_all, h_own, h_rel, h_in, dh_out, dh_rel, dh_in, eh, gh,
+    xs, w, wt, acc, unit, scale, q_all, p_all, h_own, h_rel, h_in, dh_out, dh_rel, dh_in, hw_out, hw_rel, hw_in, eh, gh,
     e_s, g_s, tile_s, csum, tq, tp, rcol, crow, rin_s, dg, dgq, dgp, lrow_s,
     dq, prt, zr, zin, dpa, dpb, a1, b1, a2, b2, ge, out_s,
     idx_s, loss_s,
-    in_sem, w_sem, send, recv, tq_send, tq_recv, tp_send, tp_recv, dg_send, dg_recv, hop_sem, pt_send, pt_recv, o_sem,
+    in_sem, w_sem, send, recv, t_sem, dg_send, dg_recv, hop_sem, o_sem,
 ):
     pb, pa = lax.axis_index("pb"), lax.axis_index("pa")
     x, y_lo = pb // 2, pb % 2
@@ -56,43 +58,52 @@
     def mod4(v):
         return (v + 8) % 4
 
-    q_slot = z * 2 + core
-    p_slot = y_hi * 8 + pb
+    q_slot = core * 8 + z
+    p_slot = y * 4 + x
+    zc = z * 2 + core
 
     def q_slot_of(zz):
         return zz * 2 + core
 
     def q_peer(s):
-        return (pb, y_hi * 16 + s)
+        return (pb, y_hi * 16 + (s % 8) * 2 + s // 8)
 
     def p_peer(s):
-        return (s % 8, (s // 8) * 16 + q_slot)
+        return device(s % 4, s // 4, z, core)
 
     def slot_of(xx, yy):
-        return (yy // 2) * 8 + xx * 2 + yy % 2
+        return yy * 4 + xx
 
     def rows(ref, slot, first=0, count=ROWS):
         return ref.at[pl.ds(pl.multiple_of(slot * ROWS + first, HALF), count)]
 
     counter = [0]
-    started = []
-
-    def remote(src, dst, to):
-        n = counter[0]
-        counter[0] += 1
-        copy = pltpu.make_async_remote_copy(
-            src_ref=src, dst_ref=dst, send_sem=send.at[n], recv_sem=recv.at[n],
+    phase = [0]
+    sent_rows = [0, 0]
+
+    def remote(src, dst, to, at=None):
+        n = counter[0] if at is None else at
+        if at is None:
+            counter[0] += 1
+        sent_rows[phase[0]] += math.prod(src.shape) // WIDTH
+        pltpu.make_async_remote_copy(
+            src_ref=src, dst_ref=dst, send_sem=send.at[phase[0]], recv_sem=recv.at[n],
             device_id=to, device_id_type=pl.DeviceIdType.MESH,
-        )
-        copy.start()
-        started.append(copy)
+        ).start()
         return n
 
     def arrive(n, dst):
         pltpu.make_async_remote_copy(
-            src_ref=dst, dst_ref=dst, send_sem=send.at[n], recv_sem=recv.at[n],
+            src_ref=dst, dst_ref=dst, send_sem=send.at[0], recv_sem=recv.at[n],
             device_id=(pb, pa), device_id_type=pl.DeviceIdType.MESH,
         ).wait_recv()
+
+    def all_sent(i):
+        part = w.at[pl.ds(0, sent_rows[i])]
+        pltpu.make_async_remote_copy(
+            src_ref=part, dst_ref=part, send_sem=send.at[i], recv_sem=recv.at[0],
+            device_id=(pb, pa), device_id_type=pl.DeviceIdType.MESH,
+        ).wait_send()
 
     inputs = []
     idx_copy = pltpu.make_async_copy(idx_ref, idx_s, in_sem.at[3])
@@ -150,20 +161,19 @@
     to_yl, to_yr, to_y2 = device(x, yl, z, core), device(x, yr, z, core), device(x, y2, z, core)
 
     def qz(zz, cc):
-        return zmod(zz) * 2 + cc
-
-    def push(ref, slot, to, first=0, count=ROWS):
+        return cc * 8 + zmod(zz)
+
+    def push(ref, slot, to, first=0, count=ROWS, at=None):
         part = rows(ref, slot, first, count)
-        return remote(part, part, to)
+        return remote(part, part, to, at)
 
     def await_rows(n, ref, slot, first=0, count=ROWS):
         arrive(n, rows(ref, slot, first, count))
 
-    other_in = []
+    SHARED, LAST = COPIES - 1, COPIES - 2
 
     def share(v, first=0, count=ROWS):
-        n = push(q_all, qz(z + v * d, core), other, first, count)
-        other_in.append((n, qz(z - v * d, 1 - core), first, count))
+        push(q_all, qz(z + v * d, core), other, first, count, SHARED)
 
     A, B = 0, HALF
     share(0)
@@ -184,11 +194,11 @@
     src_z = zmod(z - d * pb)
     src_dev = (pb, y_hi * 16 + src_z * 2 + core)
     goal_pb, goal_hi = column(y_hi * 8 + src_z)
-    goal_dev = (goal_pb, goal_hi * 16 + q_slot)
+    goal_dev = (goal_pb, goal_hi * 16 + zc)
     mine = 2 * pb + y_hi
     from_hi, from_z = mine // 8, mine % 8
     from_pb = zmod(d * (z - from_z))
-    from_dev = (from_pb, from_hi * 16 + q_slot)
+    from_dev = (from_pb, from_hi * 16 + zc)
     relays_self = pb == 0
     goal_self = jnp.logical_and(goal_pb == pb, goal_hi == y_hi)
     from_self = jnp.logical_and(from_pb == pb, from_hi == y_hi)
@@ -222,19 +232,21 @@
     h2 = (1, h_rel, h_in, goal_dev, goal_self)
     h3 = (2, dh_out, dh_rel, from_dev, from_self)
     h4 = (3, dh_rel, dh_in, src_dev, relays_self)
+    w3 = (4, hw_out, hw_rel, from_dev, from_self)
+    w4 = (5, hw_rel, hw_in, src_dev, relays_self)
 
     await_rows(p_from_xr, p_all, slot_of(xr, y))
     n_xr_yl = push(p_all, slot_of(xr, y), to_yl, A, HALF)
-    n_xr_yr = push(p_all, slot_of(xr, y), to_yr, A, HALF)
+    push(p_all, slot_of(xr, y), to_yr, A, HALF, LAST)
     await_rows(p_from_yr, p_all, slot_of(x, yr))
     m_yr_xl = push(p_all, slot_of(x, yr), to_xl, B, HALF)
-    m_yr_xr = push(p_all, slot_of(x, yr), to_xr, B, HALF)
+    push(p_all, slot_of(x, yr), to_xr, B, HALF, LAST)
     await_rows(p_from_xl, p_all, slot_of(xl, y))
     n_xl_yl = push(p_all, slot_of(xl, y), to_yl, A, HALF)
-    n_xl_yr = push(p_all, slot_of(xl, y), to_yr, A, HALF)
+    push(p_all, slot_of(xl, y), to_yr, A, HALF, LAST)
     await_rows(p_from_yl, p_all, slot_of(x, yl))
     m_yl_xl = push(p_all, slot_of(x, yl), to_xl, B, HALF)
-    m_yl_xr = push(p_all, slot_of(x, yl), to_xr, B, HALF)
+    push(p_all, slot_of(x, yl), to_xr, B, HALF, LAST)
     q4, q3l, q3s = [], [], []
     for hf in range(2):
         f = hf * HALF
@@ -251,21 +263,21 @@
     await_rows(q1s, q_all, qz(z + d, core))
     share(1)
     await_rows(p_from_x2, p_all, slot_of(x2, y))
-    n_x2_y2 = push(p_all, slot_of(x2, y), to_y2, A, HALF)
-    n_x2_yl = push(p_all, slot_of(x2, y), to_yl, A, HALF)
-    n_x2_yr = push(p_all, slot_of(x2, y), to_yr, A, HALF)
+    push(p_all, slot_of(x2, y), to_y2, A, HALF, LAST)
+    push(p_all, slot_of(x2, y), to_yl, A, HALF, LAST)
+    push(p_all, slot_of(x2, y), to_yr, A, HALF, LAST)
     await_rows(p_from_y2, p_all, slot_of(x, y2))
-    m_y2_x2 = push(p_all, slot_of(x, y2), to_x2, B, HALF)
-    m_y2_xl = push(p_all, slot_of(x, y2), to_xl, B, HALF)
-    m_y2_xr = push(p_all, slot_of(x, y2), to_xr, B, HALF)
+    push(p_all, slot_of(x, y2), to_x2, B, HALF, LAST)
+    push(p_all, slot_of(x, y2), to_xl, B, HALF, LAST)
+    push(p_all, slot_of(x, y2), to_xr, B, HALF, LAST)
     await_rows(n_xr_yl, p_all, slot_of(xr, yr), A, HALF)
-    k_xr = push(p_all, slot_of(xr, yr), to_yl, A, HALF)
+    push(p_all, slot_of(xr, yr), to_yl, A, HALF, LAST)
     await_rows(m_yr_xl, p_all, slot_of(xr, yr), B, HALF)
-    l_yr = push(p_all, slot_of(xr, yr), to_xl, B, HALF)
+    push(p_all, slot_of(xr, yr), to_xl, B, HALF, LAST)
     await_rows(n_xl_yl, p_all, slot_of(xl, yr), A, HALF)
-    k_xl = push(p_all, slot_of(xl, yr), to_yl, A, HALF)
+    push(p_all, slot_of(xl, yr), to_yl, A, HALF, LAST)
     await_rows(m_yl_xl, p_all, slot_of(xr, yl), B, HALF)
-    l_yl = push(p_all, slot_of(xr, yl), to_xl, B, HALF)
+    push(p_all, slot_of(xr, yl), to_xl, B, HALF, LAST)
     for hf in range(2):
         f = hf * HALF
         await_rows(q3s[hf], q_all, qz(z + 3 * d, core), f, HALF)
@@ -276,25 +288,10 @@
         f = hf * HALF
         await_rows(q4[hf], q_all, qz(z + 4, core), f, HALF)
         share(4, f, HALF)
-    await_rows(n_xr_yr, p_all, slot_of(xr, yl), A, HALF)
-    await_rows(n_xl_yr, p_all, slot_of(xl, yl), A, HALF)
-    await_rows(m_yr_xr, p_all, slot_of(xl, yr), B, HALF)
-    await_rows(m_yl_xr, p_all, slot_of(xl, yl), B, HALF)
-    await_rows(n_x2_y2, p_all, slot_of(x2, y2), A, HALF)
-    await_rows(m_y2_x2, p_all, slot_of(x2, y2), B, HALF)
-    await_rows(n_x2_yl, p_all, slot_of(x2, yr), A, HALF)
-    await_rows(m_y2_xl, p_all, slot_of(xr, y2), B, HALF)
-    await_rows(n_x2_yr, p_all, slot_of(x2, yl), A, HALF)
-    await_rows(m_y2_xr, p_all, slot_of(xl, y2), B, HALF)
-    await_rows(k_xr, p_all, slot_of(xr, y2), A, HALF)
-    await_rows(k_xl, p_all, slot_of(xl, y2), A, HALF)
-    await_rows(l_yr, p_all, slot_of(x2, yr), B, HALF)
-    await_rows(l_yl, p_all, slot_of(x2, yl), B, HALF)
-    for n, slot, first, count in other_in:
-        await_rows(n, q_all, slot, first, count)
-
     hop_recv(*h1)
     hop_start(*h2)
+
+    arrive(LAST, p_all.at[pl.ds(0, 14 * HALF)])
 
     csum[...] = jnp.zeros_like(csum)
 
@@ -312,52 +309,54 @@
             tq[q_slot, pl.ds(t * (TILE // 128) + j, 1), :] = row
         return carry
 
-    for t in range(GROUP // TILE):
-        score(t, 0)
+    for i in range(2):
+        score(core * 2 + i, 0)
+    arrive(SHARED, q_all.at[pl.ds(0, 8 * ROWS)])
+    for i in range(2):
+        score((1 - core) * 2 + i, 0)
     total = jnp.sum(csum[...], axis=0, keepdims=True)
     for j in range(GROUP // 128):
         tp[p_slot, pl.ds(j, 1), :] = total[:, j * 128 : (j + 1) * 128]
 
     hop_recv(*h2)
-    q_half = pl.ds(pl.multiple_of(core * 512, 512), 512)
+
+    def block_rows(j):
+        return pl.ds(pl.multiple_of((j // 2) * 512 + core * 256 + (j % 2) * 128, 128), 128)
+
+    q_half = jnp.concatenate([q_all[block_rows(j), :] for j in range(4)], axis=0)
     idx_copy.wait()
     hidx = idx_s[y_hi * 2 + core] - (from_hi * 16 + q_slot_of(from_z)) * 512 - from_pb * ROWS
-    hidx = jnp.concatenate([hidx[j : j + 1, :] for j in range(4)], axis=1)
+    hidx = jnp.concatenate(
+        [hidx[j : j + 1, c * ROWS : (c + 1) * ROWS] for c in range(2) for j in range(4)], axis=1
+    )
     named = lax.broadcasted_iota(jnp.int32, (ROWS, 512), 0) == hidx
-    e_hard = jnp.exp(inverse_temp * nt(h_in[...], q_all[q_half, :]) - inverse_temp)
+    e_hard = jnp.exp(inverse_temp * nt(h_in[...], q_half) - inverse_temp)
     e_hard = jnp.where(named, e_hard, 0.0)
     eh[...] = e_hard
+    dh_out[...] = jnp.dot(named.astype(bf16), q_half, preferred_element_type=f32).astype(bf16)
     hard_sum = jnp.sum(e_hard, axis=0, keepdims=True)
     for j in range(4):
-        tq[q_slot, pl.ds(core * 4 + j, 1), :] += hard_sum[:, j * 128 : (j + 1) * 128]
+        tq[q_slot, pl.ds((j // 2) * 4 + core * 2 + j % 2, 1), :] += hard_sum[:, j * 128 : (j + 1) * 128]
 
     eye = lax.broadcasted_iota(jnp.int32, (128, 128), 0) == lax.broadcasted_iota(jnp.int32, (128, 128), 1)
 
-    def tell(k, carry):
-        pltpu.make_async_remote_copy(
-            src_ref=tq.at[q_slot], dst_ref=tq.at[q_slot], send_sem=tq_send.at[k], recv_sem=tq_recv.at[q_slot],
-            device_id=q_peer((q_slot + k) % 16), device_id_type=pl.DeviceIdType.MESH,
-        ).start()
-        pltpu.make_async_remote_copy(
-            src_ref=tp.at[p_slot], dst_ref=tp.at[p_slot], send_sem=tp_send.at[k], recv_sem=tp_recv.at[p_slot],
-            device_id=p_peer((p_slot + k) % 16), device_id_type=pl.DeviceIdType.MESH,
-        ).start()
-        return carry
-
-    def heard(k, carry):
-        sq, sp = (q_slot + k) % 16, (p_slot + k) % 16
-        pltpu.make_async_remote_copy(
-            src_ref=tq.at[q_slot], dst_ref=tq.at[sq], send_sem=tq_send.at[k], recv_sem=tq_recv.at[sq],
-            device_id=(pb, pa), device_id_type=pl.DeviceIdType.MESH,
-        ).wait()
-        pltpu.make_async_remote_copy(
-            src_ref=tp.at[p_slot], dst_ref=tp.at[sp], send_sem=tp_send.at[k], recv_sem=tp_recv.at[sp],
-            device_id=(pb, pa), device_id_type=pl.DeviceIdType.MESH,
-        ).wait()
-        return carry
+    def total_copies(k, count):
+        first_q, first_p = (q_slot, p_slot) if count == 1 else (0, 0)
+        return [
+            pltpu.make_async_remote_copy(
+                src_ref=ref.at[pl.ds(first, count)], dst_ref=ref.at[pl.ds(first, count)],
+                send_sem=t_sem.at[2 * i], recv_sem=t_sem.at[2 * i + 1], device_id=to, device_id_type=pl.DeviceIdType.MESH,
+            )
+            for i, (ref, first, to) in enumerate(
+                ((tq, first_q, q_peer((q_slot + k) % 16)), (tp, first_p, p_peer((p_slot + k) % 16)))
+            )
+        ]
 
     for k in range(1, 16):
-        tell(k, 0)
+        for copy in total_copies(k, 1):
+            copy.start()
+
+    hop_start(*h3)
 
     is_keeper = z == mine % 8
     kb = mine // 8
@@ -366,7 +365,7 @@
     @pl.when(is_keeper)
     def _():
         for j in range(4):
-            q_rows = q_all[pl.ds(pl.multiple_of(ka * 512 + j * 128, 128), 128), :]
+            q_rows = q_all[block_rows(j), :]
             p_rows = p_all[pl.ds(pl.multiple_of(kb * 512 + j * 128, 128), 128), :]
             diag = jnp.where(eye, inverse_temp * nt(q_rows, p_rows), 0.0)
             dg[j : j + 1, :] = jnp.sum(diag, axis=0, keepdims=True)
@@ -381,7 +380,7 @@
         @pl.when(is_keeper)
         def _():
             for k in range(8):
-                sq, sp = ka * 8 + k, kb * 8 + k
+                sq, sp = (k // 4) * 8 + ka * 4 + k % 4, kb * 8 + k
 
                 @pl.when(sq != q_slot)
                 def _():
@@ -392,7 +391,7 @@
                     act(diag_copy(8 + k, dgp, p_peer(sp), 1))
 
     keep(lambda copy: copy.start())
-    dgq_self = jnp.logical_and(is_keeper, q_slot // 8 == ka)
+    dgq_self = jnp.logical_and(is_keeper, z // 4 == ka)
     dgp_self = jnp.logical_and(is_keeper, p_slot // 8 == kb)
 
     @pl.when(dgq_self)
@@ -409,8 +408,9 @@
         return carry
 
     lax.fori_loop(0, MODEL // CHUNK, turn, 0)
-    for k in range(1, 16):
-        heard(k, 0)
+    all_sent(0)
+    for copy in total_copies(1, 15):
+        copy.wait()
     sq = jnp.sum(tq[...], axis=0)
     sp = jnp.sum(tp[...], axis=0)
     rinv = inverse_temp / sq
@@ -419,10 +419,11 @@
     lrow_s[0:8, :] = sq
     lrow_s[8:16, :] = sp
 
-    hard_weight = jnp.concatenate([rin_s[pl.ds(core * 4 + j, 1), :] for j in range(4)], axis=1)
-    gh[...] = (eh[...] * hard_weight).astype(bf16)
-    dh_out[...] = jnp.dot(gh[...], q_all[q_half, :], preferred_element_type=f32).astype(bf16)
-    hop_start(*h3)
+    hard_weight = jnp.concatenate([rin_s[pl.ds((j // 2) * 4 + core * 2 + j % 2, 1), :] for j in range(4)], axis=1)
+    weighted = eh[...] * hard_weight
+    gh[...] = weighted.astype(bf16)
+    hw_out[...] = jnp.broadcast_to(jnp.sum(weighted, axis=1, keepdims=True), (ROWS, 128))
+    hop_start(*w3)
     for j in range(8):
         rcol[j * 128 : (j + 1) * 128, :] = jnp.transpose(jnp.broadcast_to(rinv[j : j + 1, :], (128, 128)))
         crow[:, j * 128 : (j + 1) * 128] = jnp.broadcast_to(cinv[j : j + 1, :], (8, 128))
@@ -431,66 +432,62 @@
     @pl.when(is_keeper)
     def _():
         for j in range(4):
-            r = pl.multiple_of(ka * 512 + j * 128, 128)
+            r = block_rows(j)
             c = pl.multiple_of(kb * 512 + j * 128, 128)
-            factor = rcol[pl.ds(r, 128), :] + crow[0:1, pl.ds(c, 128)]
-            e_s[pl.ds(r, 128), pl.ds(c, 128)] -= jnp.where(eye, 2.0 * inverse_temp / factor, 0.0)
-
-    t0 = zmod(z + 4) // 2
-
-    def question_tile(i, carry):
-        t = (t0 + i) % 4
+            factor = rcol[r, :] + crow[0:1, pl.ds(c, 128)]
+            e_s[r, pl.ds(c, 128)] -= jnp.where(eye, 2.0 * inverse_temp / factor, 0.0)
+
+    def question_tile(t):
         first = pl.multiple_of(t * TILE, TILE)
         factor = wide(rcol[pl.ds(first, TILE), :], GROUP // 128) + crow[0:1, :]
         weights = (e_s[pl.ds(first, TILE), :] * factor).astype(bf16)
         g_s[pl.ds(first, TILE), :] = weights
         value = jnp.dot(weights, p_all[...], preferred_element_type=f32)
-        here = (t // 2 == core).astype(f32)
-        value = value + here * tile_s[pl.ds(pl.multiple_of((t % 2) * TILE, TILE), TILE), :]
+        here = (t % 2 == core).astype(f32)
+        value = value + here * tile_s[pl.ds(pl.multiple_of((t // 2) * TILE, TILE), TILE), :]
         for j in range(4):
-            dq[j % 2, t * 2 + j // 2] = value[j * ROWS : (j + 1) * ROWS, :].astype(bf16)
-        pltpu.make_async_remote_copy(
-            src_ref=dq.at[1 - core, pl.ds(t * 2, 2)], dst_ref=prt.at[pl.ds(t * 2, 2)],
-            send_sem=pt_send.at[t], recv_sem=pt_recv.at[t],
-            device_id=other, device_id_type=pl.DeviceIdType.MESH,
-        ).start()
-        return carry
-
-    for i in range(4):
-        question_tile(i, 0)
-
-    def passage_tile(t, carry):
-        first = pl.multiple_of(t * TILE, TILE)
+            dq[t // 2, (t % 2) * 4 + j] = value[j * ROWS : (j + 1) * ROWS, :].astype(bf16)
+
+    def four(ref, i):
+        return ref.at[pl.ds(i * 4, 4)]
+
+    phase[0] = 1
+    n_pt = []
+    for i in range(2):
+        question_tile((1 - core) * 2 + i)
+        n_pt.append(remote(four(dq.at[1 - core], i), four(prt, i), other))
+    hop_recv(*h3)
+    hop_start(*h4)
+    for i in range(2):
+        question_tile(core * 2 + i)
+
+    def passage_tile(yy):
+        first = pl.multiple_of(yy * TILE, TILE)
         value = tn(g_s[:, pl.ds(first, TILE)], q_all[...]).astype(bf16)
         for j in range(4):
-            slot = t * 4 + j
-            yy = (slot // 8) * 2 + j % 2
-            xx = (slot % 8) // 2
-            dpa[yy, xx] = value[j * ROWS : j * ROWS + HALF, :]
-            dpb[xx, yy] = value[j * ROWS + HALF : (j + 1) * ROWS, :]
-        return carry
-
-    for t in range(2):
-        passage_tile(t, 0)
-
-    def own_sum(k, carry):
-        t = k
-        pltpu.make_async_remote_copy(
-            src_ref=dq.at[1 - core, pl.ds(t * 2, 2)], dst_ref=prt.at[pl.ds(t * 2, 2)],
-            send_sem=pt_send.at[t], recv_sem=pt_recv.at[t],
-            device_id=other, device_id_type=pl.DeviceIdType.MESH,
-        ).wait()
-        prt[pl.ds(t * 2, 2)] = (
-            prt[pl.ds(t * 2, 2)].astype(f32) + dq[core, pl.ds(t * 2, 2)].astype(f32)
-        ).astype(bf16)
-        return carry
-
-    for i in range(4):
-        own_sum((t0 + i) % 4, 0)
+            dpa[yy, j] = value[j * ROWS : j * ROWS + HALF, :]
+            dpb[j, yy] = value[j * ROWS + HALF : (j + 1) * ROWS, :]
+
+    def pair(ref, i):
+        return ref.at[pl.ds(i * 2, 2)]
 
     def half(ref, hf):
         return ref.at[pl.ds(hf * HALF, HALF)]
 
+    n_b1, n_b1s = [], []
+
+    def send_b(yy):
+        n_b1.append(remote(dpb.at[x2, yy], b1.at[0, yy], to_xr))
+        n_b1s.append(remote(dpb.at[xl, yy], b1.at[1, yy], to_xl))
+
+    passage_tile(y2)
+    n_a1 = [remote(pair(dpa.at[y2], i), pair(a1.at[0], i), to_yr) for i in range(2)]
+    send_b(y2)
+    for i in range(2):
+        arrive(n_pt[i], four(prt, i))
+        prt[i * 4 : i * 4 + 4] = (
+            prt[i * 4 : i * 4 + 4].astype(f32) + dq[core, i * 4 : i * 4 + 4].astype(f32)
+        ).astype(bf16)
     r4, r3l, r3s = [], [], []
     for hf in range(2):
         r4.append(remote(half(prt.at[zmod(z + 4)], hf), half(zr.at[0], hf), z_dev(-2 * d)))
@@ -498,17 +495,13 @@
         r3s.append(remote(half(prt.at[zmod(z + 3 * d)], hf), half(zr.at[2], hf), z_dev(d)))
     r1l = remote(prt.at[zmod(z - d)], zin.at[0], z_dev(-d))
     r1s = remote(prt.at[zmod(z + d)], zin.at[1], z_dev(d))
-
-    for t in range(2, 4):
-        passage_tile(t, 0)
-
-    def pair(ref, i):
-        return ref.at[pl.ds(i * 2, 2)]
-
-    n_a1 = [remote(pair(dpa.at[y2], i), pair(a1.at[0], i), to_yr) for i in range(2)]
-    n_b1 = [remote(pair(dpb.at[x2], i), pair(b1.at[0], i), to_xr) for i in range(2)]
+    passage_tile(yl)
     n_a1s = remote(dpa.at[yl], a1.at[1], to_yl)
-    n_b1s = remote(dpb.at[xl], b1.at[1], to_xl)
+    send_b(yl)
+    passage_tile(yr)
+    send_b(yr)
+    passage_tile(y)
+    send_b(y)
 
     n_a1l, n_b1l = [], []
     for i in range(2):
@@ -516,9 +509,6 @@
         arrive(n_a1[i], pair(a1.at[0], i))
         a1[0, two] = (a1[0, two].astype(f32) + dpa[yr, two].astype(f32)).astype(bf16)
         n_a1l.append(remote(pair(a1.at[0], i), pair(a1.at[2], i), to_yr))
-        arrive(n_b1[i], pair(b1.at[0], i))
-        b1[0, two] = (b1[0, two].astype(f32) + dpb[xr, two].astype(f32)).astype(bf16)
-        n_b1l.append(remote(pair(b1.at[0], i), pair(b1.at[2], i), to_xr))
 
     r2l, r2s = [], []
     for hf in range(2):
@@ -533,17 +523,22 @@
         ).astype(bf16)
         r2l.append(remote(half(zr.at[1], hf), half(zin.at[2], hf), z_dev(-2 * d)))
 
-    hop_recv(*h3)
-    hop_start(*h4)
+    for i, yy in enumerate((y2, yl, yr, y)):
+        arrive(n_b1[i], b1.at[0, yy])
+        b1[0, yy] = (b1[0, yy].astype(f32) + dpb[xr, yy].astype(f32)).astype(bf16)
+        n_b1l.append(remote(b1.at[0, yy], b1.at[2, yy], to_xr))
+
+    hop_recv(*w3)
+    hop_start(*w4)
 
     arrive(n_a1s, a1.at[1])
     for i in range(2):
         arrive(n_a1l[i], pair(a1.at[2], i))
     a1[1] = (a1[1].astype(f32) + a1[2].astype(f32) + dpa[y].astype(f32)).astype(bf16)
     n_a2 = [remote(a1.at[1, xx], a2.at[i], to) for i, (xx, to) in enumerate(((x2, to_x2), (xl, to_xl), (xr, to_xr)))]
-    arrive(n_b1s, b1.at[1])
-    for i in range(2):
-        arrive(n_b1l[i], pair(b1.at[2], i))
+    for i, yy in enumerate((y2, yl, yr, y)):
+        arrive(n_b1s[i], b1.at[1, yy])
+        arrive(n_b1l[i], b1.at[2, yy])
     b1[1] = (b1[1].astype(f32) + b1[2].astype(f32) + dpb[x].astype(f32)).astype(bf16)
     n_b2 = [remote(b1.at[1, yy], b2.at[i], to) for i, (yy, to) in enumerate(((y2, to_y2), (yl, to_yl), (yr, to_yr)))]
 
@@ -562,20 +557,22 @@
 
     @pl.when(jnp.logical_not(dgp_self))
     def _():
-        diag_copy(0, dgp, (group_p // 2, (group_p % 2) * 16 + q_slot), 1).wait_recv()
+        diag_copy(0, dgp, (group_p // 2, (group_p % 2) * 16 + zc), 1).wait_recv()
 
     def loss(total_row, diag, first):
         value = inverse_temp + jnp.log(total_row) - diag
         return jnp.where(first, value[:, :ROWS], value[:, ROWS:])
 
-    loss_s[0, 0:1, 0:ROWS] = loss(lrow_s[pl.ds(z, 1), :], dgq[pl.ds(z % 4, 1), :], core == 0)
-    loss_s[1, 0:1, 0:ROWS] = loss(lrow_s[pl.ds(8 + y_hi * 4 + x, 1), :], dgp[pl.ds(x, 1), :], y_lo == 0)
+    loss_s[0, 0:1, 0:ROWS] = loss(lrow_s[pl.ds(core * 4 + z // 2, 1), :], dgq[pl.ds(core * 2 + (z % 4) // 2, 1), :], z % 2 == 0)
+    loss_s[1, 0:1, 0:ROWS] = loss(lrow_s[pl.ds(8 + y * 2 + x // 2, 1), :], dgp[pl.ds(y_lo * 2 + x // 2, 1), :], x % 2 == 0)
     loss_copies = [pltpu.make_async_copy(loss_s.at[i], ref, o_sem.at[3, i]) for i, ref in enumerate((lq_ref, lp_ref))]
     for copy in loss_copies:
         copy.start()
 
     hop_recv(*h4)
-    back(dh_in[...].astype(f32), 2, 0, ROWS)
+    hop_recv(*w4)
+    grad_h = (dh_in[...].astype(f32) * wide(hw_in[...], WIDTH // 128)).astype(bf16)
+    back(grad_h.astype(f32), 2, 0, ROWS)
 
     arrive(r1l, zin.at[0])
     arrive(r1s, zin.at[1])
@@ -609,9 +606,8 @@
     for k in range(MODEL // CHUNK):
         unproject(k, 0)
 
-    for copy in started:
-        copy.wait_send()
-    for h in (h1, h2, h3, h4):
+    all_sent(1)
+    for h in (h1, h2, h3, h4, w3, w4):
         hop_sent(*h)
     keep(lambda copy: copy.wait_send())
     for k in range(MODEL // CHUNK):
@@ -639,7 +635,7 @@
         copy.wait()
 
 
-COPIES = 120
+COPIES = 130
 
 
 def shards(questions, passages, hard_rows, hard_index, projection):
@@ -669,6 +665,9 @@
             V((ROWS, WIDTH), bf16),
             V((ROWS, WIDTH), bf16),
             V((ROWS, WIDTH), bf16),
+            V((ROWS, 128), f32),
+            V((ROWS, 128), f32),
+            V((ROWS, 128), f32),
             V((ROWS, 512), f32),
             V((ROWS, 512), bf16),
             V((GROUP, GROUP), f32),
@@ -699,9 +698,9 @@
             V((4, 4, 128), jnp.int32),
             V((2, 8, 128), f32),
             D((4,)), D((MODEL // CHUNK,)),
-            D((COPIES,)), D((COPIES,)),
-            D((16,)), D((16,)), D((16,)), D((16,)),
-            D((16,)), D((2,)), D((8,)), D((4,)), D((4,)), D((4, MODEL // CHUNK)),
+            D((2,)), D((COPIES,)),
+            D((4,)),
+            D((16,)), D((2,)), D((12,)), D((4, MODEL // CHUNK)),
         ],
         compiler_params=pltpu.CompilerParams(
             collective_id=0, has_side_effects=True, vmem_limit_bytes=56 * 1024 * 1024

time: 69.7 us -> 67.2 us (0.964)
  the two profiles are of different devices: /device:TPU:36 before, /device:TPU:6 now
where the time goes in v3:
time: 67.2 us; the launch traced here: 66.7 us
  Pallas kernels  66.1 us (98%)
    pallas_call x1, Pallas kernels, shards(): pl.pallas_call(kernel, out_shape=(out, out, out, loss, loss), in_specs=[h...  63.8 us
    pallas_call x1, Pallas kernels, shards(): pl.pallas_call(hand_on, out_shape=(out, out, out, flat, flat), in_specs=(...  2.28 us

profile of v3, /device:TPU:6, one launch (start us, length us, event | category | flops | bytes accessed | tf_op | source)
XLA Modules:
  0.0 66.7 jit_solution(14357399111041436785)
XLA Ops:
  0.6 63.8 %shard_map.92 = (bf16[64,4096]{1,0:T(8,128)(2,1)}, bf16[64,4096]{1,0:T(8,128)(2,1)}, bf16[64,4096]{1,0:T(8,128)(2,1)}, f32[8,128]{1,0:T(8,128)}, f32[8,128]{1,0:T(8,128)}) custom-call(bf16[64,4096]{1,0:T(8,128)(2,1)} %xq_ref.1, bf16[64,4096]{1,0:T(8,128)(2,1)} %xp_ref.1, bf16[64,4096]{1,0:T(8,128)(2,1)} %xh_ref.1, s32[4,4,128]{2,1,0:T(4,128)} %bitcast.1, ...), custom_call_target="tpu_custom_call" | custom-call | flops 8000000000 | bytes 10000000 | tf_op jit(solution)/shard_map/pallas_call | solution.py:648
  64.4 2.3 %shard_map.93 = (bf16[64,4096]{1,0:T(8,128)(2,1)}, bf16[64,4096]{1,0:T(8,128)(2,1)}, bf16[64,4096]{1,0:T(8,128)(2,1)}, f32[64]{0:T(128)}, f32[64]{0:T(128)}) custom-call(bf16[64,4096]{1,0:T(8,128)(2,1)} %get-tuple-element.10.gq, bf16[64,4096]{1,0:T(8,128)(2,1)} %get-tuple-element.11.gp, bf16[64,4096]{1,0:T(8,128)(2,1)} %get-tuple-element.12.gh, ...), custom_call_target="tpu_custom_call" | custom-call | bytes 3000000 | tf_op jit(solution)/shard_map/pallas_call | solution.py:710

commit v4 on v3

--- a/solution.py
+++ b/solution.py
@@ -234,6 +234,8 @@
     h4 = (3, dh_rel, dh_in, src_dev, relays_self)
     w3 = (4, hw_out, hw_rel, from_dev, from_self)
     w4 = (5, hw_rel, hw_in, src_dev, relays_self)
+
+    hop_start(*h1)
 
     await_rows(p_from_xr, p_all, slot_of(xr, y))
     n_xr_yl = push(p_all, slot_of(xr, y), to_yl, A, HALF)
@@ -257,7 +259,6 @@
         await_rows(q2[hf][1], q_all, qz(z + 2 * d, core), f, HALF)
         share(2, f, HALF)
         q3s.append(push(q_all, qz(z + 2 * d, core), z_dev(-d), f, HALF))
-    hop_start(*h1)
     await_rows(q1l, q_all, qz(z - d, core))
     share(-1)
     await_rows(q1s, q_all, qz(z + d, core))
@@ -278,6 +279,8 @@
     push(p_all, slot_of(xl, yr), to_yl, A, HALF, LAST)
     await_rows(m_yl_xl, p_all, slot_of(xr, yl), B, HALF)
     push(p_all, slot_of(xr, yl), to_xl, B, HALF, LAST)
+    hop_recv(*h1)
+    hop_start(*h2)
     for hf in range(2):
         f = hf * HALF
         await_rows(q3s[hf], q_all, qz(z + 3 * d, core), f, HALF)
@@ -288,8 +291,6 @@
         f = hf * HALF
         await_rows(q4[hf], q_all, qz(z + 4, core), f, HALF)
         share(4, f, HALF)
-    hop_recv(*h1)
-    hop_start(*h2)
 
     arrive(LAST, p_all.at[pl.ds(0, 14 * HALF)])
 
@@ -318,28 +319,6 @@
     for j in range(GROUP // 128):
         tp[p_slot, pl.ds(j, 1), :] = total[:, j * 128 : (j + 1) * 128]
 
-    hop_recv(*h2)
-
-    def block_rows(j):
-        return pl.ds(pl.multiple_of((j // 2) * 512 + core * 256 + (j % 2) * 128, 128), 128)
-
-    q_half = jnp.concatenate([q_all[block_rows(j), :] for j in range(4)], axis=0)
-    idx_copy.wait()
-    hidx = idx_s[y_hi * 2 + core] - (from_hi * 16 + q_slot_of(from_z)) * 512 - from_pb * ROWS
-    hidx = jnp.concatenate(
-        [hidx[j : j + 1, c * ROWS : (c + 1) * ROWS] for c in range(2) for j in range(4)], axis=1
-    )
-    named = lax.broadcasted_iota(jnp.int32, (ROWS, 512), 0) == hidx
-    e_hard = jnp.exp(inverse_temp * nt(h_in[...], q_half) - inverse_temp)
-    e_hard = jnp.where(named, e_hard, 0.0)
-    eh[...] = e_hard
-    dh_out[...] = jnp.dot(named.astype(bf16), q_half, preferred_element_type=f32).astype(bf16)
-    hard_sum = jnp.sum(e_hard, axis=0, keepdims=True)
-    for j in range(4):
-        tq[q_slot, pl.ds((j // 2) * 4 + core * 2 + j % 2, 1), :] += hard_sum[:, j * 128 : (j + 1) * 128]
-
-    eye = lax.broadcasted_iota(jnp.int32, (128, 128), 0) == lax.broadcasted_iota(jnp.int32, (128, 128), 1)
-
     def total_copies(k, count):
         first_q, first_p = (q_slot, p_slot) if count == 1 else (0, 0)
         return [
@@ -352,10 +331,34 @@
             )
         ]
 
-    for k in range(1, 16):
-        for copy in total_copies(k, 1):
-            copy.start()
-
+    for k in (10, 9, 11, 6, 14, 2, 8, 5, 7, 13, 15, 1, 3, 4, 12):
+        total_copies(k, 1)[1].start()
+
+    hop_recv(*h2)
+
+    def block_rows(j):
+        return pl.ds(pl.multiple_of((j // 2) * 512 + core * 256 + (j % 2) * 128, 128), 128)
+
+    q_half = jnp.concatenate([q_all[block_rows(j), :] for j in range(4)], axis=0)
+    idx_copy.wait()
+    hidx = idx_s[y_hi * 2 + core] - (from_hi * 16 + q_slot_of(from_z)) * 512 - from_pb * ROWS
+    hidx = jnp.concatenate(
+        [hidx[j : j + 1, c * ROWS : (c + 1) * ROWS] for c in range(2) for j in range(4)], axis=1
+    )
+    named = lax.broadcasted_iota(jnp.int32, (ROWS, 512), 0) == hidx
+    e_hard = jnp.exp(inverse_temp * nt(h_in[...], q_half) - inverse_temp)
+    e_hard = jnp.where(named, e_hard, 0.0)
+    eh[...] = e_hard
+    hard_sum = jnp.sum(e_hard, axis=0, keepdims=True)
+    for j in range(4):
+        tq[q_slot, pl.ds((j // 2) * 4 + core * 2 + j % 2, 1), :] += hard_sum[:, j * 128 : (j + 1) * 128]
+
+    eye = lax.broadcasted_iota(jnp.int32, (128, 128), 0) == lax.broadcasted_iota(jnp.int32, (128, 128), 1)
+
+    for k in (4, 12, 5, 3, 11, 13, 6, 2, 10, 14, 7, 1, 9, 15, 8):
+        total_copies(k, 1)[0].start()
+
+    dh_out[...] = jnp.dot(named.astype(bf16), q_half, preferred_element_type=f32).astype(bf16)
     hop_start(*h3)
 
     is_keeper = z == mine % 8
@@ -511,7 +514,7 @@
         n_a1l.append(remote(pair(a1.at[0], i), pair(a1.at[2], i), to_yr))
 
     r2l, r2s = [], []
-    for hf in range(2):
+    def q_relay(hf):
         part = slice(hf * HALF, (hf + 1) * HALF)
         arrive(r3s[hf], half(zr.at[2], hf))
         zr[2, part, :] = (zr[2, part, :].astype(f32) + prt[zmod(z + 2 * d), part, :].astype(f32)).astype(bf16)
@@ -523,10 +526,17 @@
         ).astype(bf16)
         r2l.append(remote(half(zr.at[1], hf), half(zin.at[2], hf), z_dev(-2 * d)))
 
-    for i, yy in enumerate((y2, yl, yr, y)):
+    def b_relay(i, yy):
         arrive(n_b1[i], b1.at[0, yy])
         b1[0, yy] = (b1[0, yy].astype(f32) + dpb[xr, yy].astype(f32)).astype(bf16)
         n_b1l.append(remote(b1.at[0, yy], b1.at[2, yy], to_xr))
+
+    b_relay(0, y2)
+    b_relay(1, yl)
+    q_relay(0)
+    b_relay(2, yr)
+    b_relay(3, y)
+    q_relay(1)
 
     hop_recv(*w3)
     hop_start(*w4)

time: 67.2 us -> 63 us (0.938)
  Pallas kernels: 66.1 us -> 62.2 us
    pallas_call x1, Pallas kernels: 63.8 us -> 59.9 us  [shards(): pl.pallas_call(kernel, out_shape=(out, out, out, loss, loss), in_specs=[h...]
where the time goes in v4:
time: 63 us; the launch traced here: 62.8 us
  Pallas kernels  62.2 us (99%)
  between operations  0.64 us (1%)
    pallas_call x1, Pallas kernels, shards(): pl.pallas_call(kernel, out_shape=(out, out, out, loss, loss), in_specs=[h...  59.9 us
    pallas_call x1, Pallas kernels, shards(): pl.pallas_call(hand_on, out_shape=(out, out, out, flat, flat), in_specs=(...  2.28 us

profile of v4, /device:TPU:6, one launch (start us, length us, event | category | flops | bytes accessed | tf_op | source)
XLA Modules:
  0.0 62.8 jit_solution(15036857616929039310)
XLA Ops:
  0.6 59.9 %shard_map.92 = (bf16[64,4096]{1,0:T(8,128)(2,1)}, bf16[64,4096]{1,0:T(8,128)(2,1)}, bf16[64,4096]{1,0:T(8,128)(2,1)}, f32[8,128]{1,0:T(8,128)}, f32[8,128]{1,0:T(8,128)}) custom-call(bf16[64,4096]{1,0:T(8,128)(2,1)} %xq_ref.1, bf16[64,4096]{1,0:T(8,128)(2,1)} %xp_ref.1, bf16[64,4096]{1,0:T(8,128)(2,1)} %xh_ref.1, s32[4,4,128]{2,1,0:T(4,128)} %bitcast.1, ...), custom_call_target="tpu_custom_call" | custom-call | flops 8000000000 | bytes 10000000 | tf_op jit(solution)/shard_map/pallas_call | solution.py:658
  60.6 2.3 %shard_map.93 = (bf16[64,4096]{1,0:T(8,128)(2,1)}, bf16[64,4096]{1,0:T(8,128)(2,1)}, bf16[64,4096]{1,0:T(8,128)(2,1)}, f32[64]{0:T(128)}, f32[64]{0:T(128)}) custom-call(bf16[64,4096]{1,0:T(8,128)(2,1)} %get-tuple-element.10.gq, bf16[64,4096]{1,0:T(8,128)(2,1)} %get-tuple-element.11.gp, bf16[64,4096]{1,0:T(8,128)(2,1)} %get-tuple-element.12.gh, ...), custom_call_target="tpu_custom_call" | custom-call | bytes 3000000 | tf_op jit(solution)/shard_map/pallas_call | solution.py:720

commit v5 on v4

--- a/solution.py
+++ b/solution.py
@@ -237,20 +237,9 @@
 
     hop_start(*h1)
 
-    await_rows(p_from_xr, p_all, slot_of(xr, y))
-    n_xr_yl = push(p_all, slot_of(xr, y), to_yl, A, HALF)
-    push(p_all, slot_of(xr, y), to_yr, A, HALF, LAST)
-    await_rows(p_from_yr, p_all, slot_of(x, yr))
-    m_yr_xl = push(p_all, slot_of(x, yr), to_xl, B, HALF)
-    push(p_all, slot_of(x, yr), to_xr, B, HALF, LAST)
-    await_rows(p_from_xl, p_all, slot_of(xl, y))
-    n_xl_yl = push(p_all, slot_of(xl, y), to_yl, A, HALF)
-    push(p_all, slot_of(xl, y), to_yr, A, HALF, LAST)
-    await_rows(p_from_yl, p_all, slot_of(x, yl))
-    m_yl_xl = push(p_all, slot_of(x, yl), to_xl, B, HALF)
-    push(p_all, slot_of(x, yl), to_xr, B, HALF, LAST)
     q4, q3l, q3s = [], [], []
-    for hf in range(2):
+
+    def q_pass(hf):
         f = hf * HALF
         await_rows(q2[hf][0], q_all, qz(z - 2 * d, core), f, HALF)
         share(-2, f, HALF)
@@ -259,6 +248,21 @@
         await_rows(q2[hf][1], q_all, qz(z + 2 * d, core), f, HALF)
         share(2, f, HALF)
         q3s.append(push(q_all, qz(z + 2 * d, core), z_dev(-d), f, HALF))
+
+    q_pass(0)
+    await_rows(p_from_xr, p_all, slot_of(xr, y))
+    n_xr_yl = push(p_all, slot_of(xr, y), to_yl, A, HALF)
+    push(p_all, slot_of(xr, y), to_yr, A, HALF, LAST)
+    await_rows(p_from_yr, p_all, slot_of(x, yr))
+    m_yr_xl = push(p_all, slot_of(x, yr), to_xl, B, HALF)
+    push(p_all, slot_of(x, yr), to_xr, B, HALF, LAST)
+    q_pass(1)
+    await_rows(p_from_xl, p_all, slot_of(xl, y))
+    n_xl_yl = push(p_all, slot_of(xl, y), to_yl, A, HALF)
+    push(p_all, slot_of(xl, y), to_yr, A, HALF, LAST)
+    await_rows(p_from_yl, p_all, slot_of(x, yl))
+    m_yl_xl = push(p_all, slot_of(x, yl), to_xl, B, HALF)
+    push(p_all, slot_of(x, yl), to_xr, B, HALF, LAST)
     await_rows(q1l, q_all, qz(z - d, core))
     share(-1)
     await_rows(q1s, q_all, qz(z + d, core))

time: 63 us -> 62.5 us (level)
  no operation moved by 1% of the time
where the time goes in v5:
time: 62.5 us; the launch traced here: 62.3 us
  Pallas kernels  61.7 us (99%)
  between operations  0.64 us (1%)
    pallas_call x1, Pallas kernels, shards(): pl.pallas_call(kernel, out_shape=(out, out, out, loss, loss), in_specs=[h...  59.4 us
    pallas_call x1, Pallas kernels, shards(): pl.pallas_call(hand_on, out_shape=(out, out, out, flat, flat), in_specs=(...  2.28 us

profile of v5, /device:TPU:6, one launch (start us, length us, event | category | flops | bytes accessed | tf_op | source)
XLA Modules:
  0.0 62.3 jit_solution(11921073268347819847)
XLA Ops:
  0.6 59.4 %shard_map.92 = (bf16[64,4096]{1,0:T(8,128)(2,1)}, bf16[64,4096]{1,0:T(8,128)(2,1)}, bf16[64,4096]{1,0:T(8,128)(2,1)}, f32[8,128]{1,0:T(8,128)}, f32[8,128]{1,0:T(8,128)}) custom-call(bf16[64,4096]{1,0:T(8,128)(2,1)} %xq_ref.1, bf16[64,4096]{1,0:T(8,128)(2,1)} %xp_ref.1, bf16[64,4096]{1,0:T(8,128)(2,1)} %xh_ref.1, s32[4,4,128]{2,1,0:T(4,128)} %bitcast.1, ...), custom_call_target="tpu_custom_call" | custom-call | flops 8000000000 | bytes 10000000 | tf_op jit(solution)/shard_map/pallas_call | solution.py:662
  60.0 2.3 %shard_map.93 = (bf16[64,4096]{1,0:T(8,128)(2,1)}, bf16[64,4096]{1,0:T(8,128)(2,1)}, bf16[64,4096]{1,0:T(8,128)(2,1)}, f32[64]{0:T(128)}, f32[64]{0:T(128)}) custom-call(bf16[64,4096]{1,0:T(8,128)(2,1)} %get-tuple-element.10.gq, bf16[64,4096]{1,0:T(8,128)(2,1)} %get-tuple-element.11.gp, bf16[64,4096]{1,0:T(8,128)(2,1)} %get-tuple-element.12.gh, ...), custom_call_target="tpu_custom_call" | custom-call | bytes 3000000 | tf_op jit(solution)/shard_map/pallas_call | solution.py:724
